TPU v7x, 256 devices: a whole 4x4x8 slice. The times are simulated.
256 devices in a mesh: batch: 8 (over z_hi, y), dap: 32 (over z_lo, x, core).
Axes of the slice: x: 4, y: 4, z: 8 (z_hi: 2, z_lo: 4; z = z_hi * 4 + z_lo), core: 2. Of those that a mesh axis runs over, the one named last changes fastest.
Arguments:
- relative_embedding: bfloat16 [4096, 256, 256], P(('batch', 'dap')), parts along dimension 0, may hold values from -6 to 6
- coupling_features: bfloat16 [2048, 256, 128], P(('batch', 'dap')), parts along dimension 0, may hold values from -6 to 6
- relative_variance_multiplier: float32 [256], replicated, may hold values from 0.1 to 1.9
- bilinear_lhs_projector: bfloat16 [256, 32], replicated, may hold values from -0.375 to 0.375
- bilinear_rhs_projector: bfloat16 [256, 32], replicated, may hold values from -0.375 to 0.375
- product_final_matrix: bfloat16 [1024, 128], replicated, may hold values from -4 to 4
- coupling_standard_scale: float32 [128], replicated, may hold values from 0.1 to 1.9
- incoming_edge_matrix: bfloat16 [128, 128], replicated, may hold values from -0.5 to 0.5
- incoming_edge_sigmoid: bfloat16 [128, 128], replicated, may hold values from -0.5 to 0.5
- second_edge_matrix: bfloat16 [128, 128], replicated, may hold values from -0.5 to 0.5
- second_edge_sigmoid: bfloat16 [128, 128], replicated, may hold values from -0.5 to 0.5
- update_sigmoid_matrix: bfloat16 [128, 128], replicated, may hold values from -0.5 to 0.5
- update_final_matrix: bfloat16 [128, 128], replicated, may hold values from -0.5 to 0.5
- cubic_standard_scale: float32 [128], replicated, may hold values from 0.1 to 1.9
Outputs:
- pair_out: bfloat16 [2048, 256, 128], P(('batch', 'dap')), parts along dimension 0
There are 8 independent parts, one for each index of `batch`. A program takes and returns all parts, laid end to end along the dimension named above; an argument that names none is the same for every part. Nothing has to cross between parts.
All inputs are finite; a program needn't handle non-finite values.
Results may differ from a plain program's by a relative error of at most 0.0075.
Values may be sent and summed in bfloat16 or wider, within the bound.
A program may use at most 128 MiB of HBM per device.

v0:
```python
import jax
import jax.numpy as jnp
from jax import lax
from jax.sharding import PartitionSpec as P


def standardize_features(values, gain):
    mean = jnp.mean(values, axis=-1, keepdims=True)
    centred = values - mean
    spread = jnp.mean(centred * centred, axis=-1, keepdims=True)
    return centred * lax.rsqrt(spread + 1e-05) * gain


def gated_edge(normed, weight, gate):
    opened = jax.nn.sigmoid(jnp.dot(normed, gate, preferred_element_type=jnp.float32))
    return (opened * jnp.dot(normed, weight, preferred_element_type=jnp.float32)).astype(
        jnp.bfloat16
    )


def local(
    relative_embedding,
    coupling_features,
    relative_variance_multiplier,
    bilinear_lhs_projector,
    bilinear_rhs_projector,
    product_final_matrix,
    coupling_standard_scale,
    incoming_edge_matrix,
    incoming_edge_sigmoid,
    second_edge_matrix,
    second_edge_sigmoid,
    update_sigmoid_matrix,
    update_final_matrix,
    cubic_standard_scale,
):
    homolog_standardized = standardize_features(
        relative_embedding.astype(jnp.float32), relative_variance_multiplier
    ).astype(jnp.bfloat16)
    left_factor = jnp.dot(
        homolog_standardized, bilinear_lhs_projector, preferred_element_type=jnp.float32
    ).astype(jnp.bfloat16)
    right_factor = jnp.dot(
        homolog_standardized, bilinear_rhs_projector, preferred_element_type=jnp.float32
    ).astype(jnp.bfloat16)
    my_rows = coupling_features.shape[0]
    flat_width = product_final_matrix.shape[0]
    left_res, right_res = (
        lax.all_to_all(left_factor, "dap", split_axis=1, concat_axis=0, tiled=True),
        lax.all_to_all(right_factor, "dap", split_axis=1, concat_axis=0, tiled=True),
    )
    total = left_res.shape[0]
    piece = lax.all_gather(right_res, "dap", axis=1, tiled=True)
    outer = jnp.einsum("sic,sjd->ijcd", left_res, piece, preferred_element_type=jnp.float32) * (
        1.0 / total
    )
    outer = outer.astype(jnp.bfloat16).reshape(my_rows, piece.shape[1], flat_width)
    update = jnp.dot(outer, product_final_matrix, preferred_element_type=jnp.float32)
    pair_mid = coupling_features.astype(jnp.float32) + update
    pair_norm = standardize_features(pair_mid, coupling_standard_scale).astype(jnp.bfloat16)
    edge_left = gated_edge(pair_norm, incoming_edge_matrix, incoming_edge_sigmoid)
    edge_right = gated_edge(pair_norm, second_edge_matrix, second_edge_sigmoid)
    tri = jnp.einsum(
        "ikc,jkc->ijc",
        edge_left,
        lax.all_gather(edge_right, "dap", axis=0, tiled=True),
        preferred_element_type=jnp.float32,
    )
    tri_norm = standardize_features(tri, cubic_standard_scale).astype(jnp.bfloat16)
    opened = jax.nn.sigmoid(
        jnp.dot(pair_norm, update_sigmoid_matrix, preferred_element_type=jnp.float32)
    )
    result = pair_mid + opened * jnp.dot(
        tri_norm, update_final_matrix, preferred_element_type=jnp.float32
    )
    return result.astype(jnp.bfloat16)


def solution(mesh):
    return jax.shard_map(
        local,
        mesh=mesh,
        in_specs=(
            P(("batch", "dap"), None, None),
            P(("batch", "dap"), None, None),
            P(),
            P(),
            P(),
            P(),
            P(),
            P(),
            P(),
            P(),
            P(),
            P(),
            P(),
            P(),
        ),
        out_specs=P(("batch", "dap"), None, None),
        check_vma=False,
    )
```

profile of v0, /device:TPU:1, one launch (start us, length us, event | category | flops | bytes accessed | tf_op | source)
XLA Modules:
  0.0 265.6 jit_solution(4225083303306155224)
XLA Ops:
  6.6 2.4 convert_reduce_fusion
  9.0 2.5 fusion.4
  11.5 2.2 fusion.30
  13.7 1.9 copy.44
  15.6 1.7 reshape.54
  17.4 21.2 %all_to_all.36 = bf16[32,2,2048]{2,1,0:T(2,128)(2,1)} all-to-all(bf16[32,2,2048]{2,1,0:T(2,128)(2,1)} %reshape.54), channel_id=1, replica_groups=mesh['batch'=8,'dap'=32] {'dap'}, dimensions={0} | all-to-all | bytes 524288 | tf_op jit(solution)/shard_map/all_to_all | solution.py:50
  38.6 1.9 reshape.55
  40.5 1.2 copy.46
  41.8 2.8 %copy.47 = bf16[512,8,32]{0,1,2:T(8,128)(2,1)} copy(bf16[512,8,32]{2,1,0:T(8,128)(2,1)} %bitcast.67) | data formatting | bytes 524288 | tf_op jit(solution)/shard_map/all_to_all | solution.py:50
  44.6 1.9 fusion.33
  46.5 1.0 copy.48
  47.5 1.7 reshape.56
  49.2 3.8 %all-to-all-start.1 = ((bf16[32,2,2048]{2,1,0:T(2,128)(2,1)}), bf16[32,2,2048]{2,1,0:T(2,128)(2,1)S(1)}, u32[]{:S(2)}, u32[]{:S(2)}) async-start(bf16[32,2,2048]{2,1,0:T(2,128)(2,1)} %reshape.56), calls=%async_computation.1 | async-start | bytes 524288 | tf_op jit(solution)/shard_map/all_to_all | solution.py:49
  53.5 13.5 %all-to-all-done.1 = bf16[32,2,2048]{2,1,0:T(2,128)(2,1)S(1)} async-done(((bf16[32,2,2048]{2,1,0:T(2,128)(2,1)}), bf16[32,2,2048]{2,1,0:T(2,128)(2,1)S(1)}, u32[]{:S(2)}, u32[]{:S(2)}) %all-to-all-start.1) | async-done | bytes 262176 | tf_op jit(solution)/shard_map/all_to_all | solution.py:49
  67.0 0.5 reshape.57
  67.5 0.3 copy.50
  67.8 0.7 copy.51
  68.5 46.5 %all-gather.3.cloned.1.call-done = bf16[512,256,32]{0,1,2:T(8,128)(2,1)} async-done(((bf16[512,8,32]{0,1,2:T(8,128)(2,1)}), bf16[512,256,32]{0,1,2:T(8,128)(2,1)}) %all-gather.3.cloned.1.call-update) | async-done | bytes 8388624 | tf_op jit(solution)/shard_map/all_gather | solution.py:53
  115.0 5.8 %fusion.7 = bf16[8,256,32,32]{1,2,0,3:T(8,128)(2,1)S(1)} fusion(bf16[512,256,32]{0,1,2:T(8,128)(2,1)} %all-gather.3.cloned.1.call-done, bf16[512,8,32]{0,2,1:T(8,128)(2,1)S(1)} %copy.51), kind=kOutput, calls=%fused_computation.10 | convolution fusion | flops 2151677952 | bytes 12845056 | tf_op jit(solution)/shard_map/sic,sjd->ijcd/dot_general | solution.py:54
  120.7 2.6 copy.52
  123.4 0.8 fusion.51
  124.5 0.3 fusion.45
  124.9 0.5 fusion.28
  125.4 1.0 copy.61
  126.4 0.3 fusion.42
  126.8 0.5 fusion.27
  127.3 98.7 %all-gather.5.cloned.1.call-done = bf16[256,256,128]{2,1,0:T(8,128)(2,1)} async-done(((bf16[8,256,128]{2,1,0:T(8,128)(2,1)}), bf16[256,256,128]{2,1,0:T(8,128)(2,1)}) %all-gather.5.cloned.1.call-update) | async-done | bytes 16777232 | tf_op jit(solution)/shard_map/all_gather | solution.py:66
  226.0 22.3 %copy.66 = bf16[256,256,128]{1,0,2:T(8,128)(2,1)} copy(bf16[256,256,128]{2,1,0:T(8,128)(2,1)} %all-gather.5.cloned.1.call-done) | data formatting | bytes 33554432 | tf_op jit(solution)/shard_map/all_gather | solution.py:66
  248.3 8.1 %fusion.52 = (f32[8,256]{1,0:T(8,128)S(1)}, f32[8,256,128]{1,0,2:T(8,128)S(1)}) fusion(bf16[256,256,128]{1,0,2:T(8,128)(2,1)} %copy.66, bf16[8,256,128]{1,2,0:T(8,128)(2,1)S(1)} %fusion.27), kind=kOutput, calls=%fused_computation.62 | convolution fusion | flops 134477824 | bytes 18358272 | tf_op jit(solution)/shard_map/ikc,jkc->ijc/dot_general | solution.py:63
  256.8 0.3 fusion.36
  257.1 0.6 fusion.29
  257.7 1.0 copy.70
  (45 shorter events, 1.3 us)
Async XLA Ops:
  6.5 116.8 %copy-start = (bf16[1024,128]{1,0:T(8,128)(2,1)S(1)}, bf16[1024,128]{1,0:T(8,128)(2,1)}, u32[]{:S(2)}) copy-start(bf16[1024,128]{1,0:T(8,128)(2,1)} %param.19) | copy-start | bytes 786436
  6.5 5.0 %copy-start.2 = (bf16[16,256,256]{2,1,0:T(8,128)(2,1)S(1)}, bf16[16,256,256]{2,1,0:T(8,128)(2,1)}, u32[]{:S(2)}) copy-start(bf16[16,256,256]{2,1,0:T(8,128)(2,1)} %param.14) | copy-start | bytes 6291460
  6.5 5.0 %copy-start.14 = (f32[256]{0:T(256)S(1)}, f32[256]{0:T(256)}, u32[]{:S(2)}) copy-start(f32[256]{0:T(256)} %param.16) | copy-start | bytes 3076
  6.5 5.0 %copy-start.12 = (bf16[256,32]{0,1:T(8,128)(2,1)S(1)}, bf16[256,32]{0,1:T(8,128)(2,1)}, u32[]{:S(2)}) copy-start(bf16[256,32]{0,1:T(8,128)(2,1)} %param.18) | copy-start | bytes 49156
  6.5 108.4 %all-gather.3.cloned.1.call-start = ((), (), s32[]{:S(2)}) async-start(), calls=%async_computation.2 | async-start | bytes 8650752 | tf_op jit(solution)/shard_map/all_gather | solution.py:53
  13.7 30.9 %copy-start.13 = (bf16[256,32]{0,1:T(8,128)(2,1)S(1)}, bf16[256,32]{0,1:T(8,128)(2,1)}, u32[]{:S(2)}) copy-start(bf16[256,32]{0,1:T(8,128)(2,1)} %param.17) | copy-start | bytes 49156
  44.6 8.7 %copy-start.3 = (bf16[8,256,128]{2,1,0:T(8,128)(2,1)S(1)}, bf16[8,256,128]{2,1,0:T(8,128)(2,1)}, u32[]{:S(2)}) copy-start(bf16[8,256,128]{2,1,0:T(8,128)(2,1)} %param.15) | copy-start | bytes 1572868
  49.2 17.8 %all-to-all-start.1 = ((bf16[32,2,2048]{2,1,0:T(2,128)(2,1)}), bf16[32,2,2048]{2,1,0:T(2,128)(2,1)S(1)}, u32[]{:S(2)}, u32[]{:S(2)}) async-start(bf16[32,2,2048]{2,1,0:T(2,128)(2,1)} %reshape.56), calls=%async_computation.1 | async-start | bytes 524288 | tf_op jit(solution)/shard_map/all_to_all | solution.py:49
  53.0 172.9 %all-gather.5.cloned.1.call-start = ((), (), s32[]{:S(2)}) async-start(), calls=%async_computation.3 | async-start | bytes 17301504 | tf_op jit(solution)/shard_map/all_gather | solution.py:66
  123.4 1.0 copy-start.7
  123.4 1.1 copy-start.4
  123.4 1.5 copy-start.9
  124.5 1.9 copy-start.5
  124.9 1.9 copy-start.10
  248.3 8.3 %copy-start.8 = (f32[128]{0:T(128)S(1)}, f32[128]{0:T(128)}, u32[]{:S(2)}) copy-start(f32[128]{0:T(128)} %param.27) | copy-start | bytes 1540
  248.3 8.5 %copy-start.6 = (bf16[128,128]{1,0:T(8,128)(2,1)S(1)}, bf16[128,128]{1,0:T(8,128)(2,1)}, u32[]{:S(2)}) copy-start(bf16[128,128]{1,0:T(8,128)(2,1)} %param.26) | copy-start | bytes 98308
  256.3 0.8 copy-start.11
  256.5 2.2 copy-start.1
Sparse Core Ops, SparseCore 0:
  44.7 70.1 all-gather.2
  126.6 99.3 all-gather.4
where the time goes:
time: 266 us
  waiting for transfers between devices  159 us (60%)
  local copies, waits for them, and re-layouts  41 us (15%)
  matrix products  21.3 us (8%)
  blocking collectives  21.2 us (8%)
  between operations  13.8 us (5%)
  other arithmetic  5.58 us (2%)
  starting transfers between devices  4.08 us (2%)
    all_gather x1, waiting for transfers between devices, local(): lax.all_gather(edge_right, 'dap', axis=0, tiled=True)  98.7 us
    all_gather x1, waiting for transfers between devices, local(): piece = lax.all_gather(right_res, 'dap', axis=1, tiled=True)  46.5 us
    all_gather x1, local copies, waits for them, and re-layouts, local(): lax.all_gather(edge_right, 'dap', axis=0, tiled=True)  22.3 us
    all_to_all x1, blocking collectives, local(): lax.all_to_all(right_factor, 'dap', split_axis=1, concat_axis=0, tiled=True)  21.2 us
    all_to_all x1, waiting for transfers between devices, local(): lax.all_to_all(left_factor, 'dap', split_axis=1, concat_axis=0, tiled=True)  13.5 us
    dot_general x1, matrix products, local(): jnp.einsum('ikc,jkc->ijc', edge_left, lax.all_gather(edge_right, 'dap', a...  8.08 us
    unnamed x35, local copies, waits for them, and re-layouts  6.18 us
    dot_general x1, matrix products, local(): jnp.einsum('sic,sjd->ijcd', left_res, piece, preferred_element_type=jnp.f...  5.75 us
  transfers between devices with their start and end apart: 3, of which 3 were waited for; matrix products, arithmetic and copies ran while one was open for 3% of the time, Pallas kernels for 0%

commit v1 on v0

v1 whole, which is shorter than its diff:
```python
import jax
import jax.numpy as jnp
from jax import lax
from jax.experimental import pallas as pl
from jax.experimental.pallas import tpu as pltpu
from jax.sharding import PartitionSpec as P

MESH = pl.DeviceIdType.MESH
F32 = jnp.float32
BF16 = jnp.bfloat16
CHUNKS = 4
ND = 32 // CHUNKS
NT = (((1,), (1,)), ((), ()))


def remote(src, dst, send_sem, recv_sem, target):
    return pltpu.make_async_remote_copy(
        src_ref=src,
        dst_ref=dst,
        send_sem=send_sem,
        recv_sem=recv_sem,
        device_id={"dap": target},
        device_id_type=MESH,
    )


def column(row):
    return jnp.broadcast_to(row, (128, 128)).T


def norm_rows(v, gain):
    mean = jnp.mean(v, axis=0, keepdims=True)
    centred = v - mean
    spread = jnp.mean(centred * centred, axis=0, keepdims=True)
    return (centred * lax.rsqrt(spread + 1e-05) * gain).astype(BF16)


def kernel(
    msa,
    coup,
    msa_gain,
    w_lhs,
    w_rhs,
    w_final,
    pair_gain,
    w_el,
    g_el,
    w_er,
    g_er,
    g_up,
    w_up,
    tri_gain,
    out,
    s_left,
    s_right,
    l_send,
    l_all,
    l_t,
    r_send,
    r_all,
    outer,
    coup16,
    w2,
    w5,
    wu,
    mid,
    gate,
    s_el,
    s_er,
    e_send,
    e_recv,
    t_send,
    t_recv,
    s_tri,
    o_buf,
    o_got,
    sib_send,
    sib_recv,
    l_ssem,
    l_rsem,
    z_ssem,
    x_ssem,
    f_ssem,
    r_rsem,
    f_rsem,
    e_ssem,
    e_rsem,
    t_ssem,
    t_rsem,
):
    me = lax.axis_index("dap")
    h = me % 2
    q = me // 2
    x = q % 4
    z = q // 4
    sib = 2 * q + (1 - h)

    def dev(zz, xx):
        return 2 * (4 * zz + xx) + h

    barrier = pltpu.get_barrier_semaphore()

    @pl.loop(1, 32)
    def _(k):
        pl.semaphore_signal(
            barrier, inc=1, device_id={"dap": (me + k) % 32}, device_id_type=MESH
        )

    wl4 = jnp.concatenate([w_lhs[...]] * 4, axis=1)
    wrt = w_rhs[...].astype(F32).T.astype(BF16)
    gain = msa_gain[...]

    @pl.loop(0, 16)
    def _(s):
        v = msa[s].astype(F32)
        mean = jnp.mean(v, axis=-1, keepdims=True)
        centred = v - mean
        spread = jnp.mean(centred * centred, axis=-1, keepdims=True)
        normed = (centred * lax.rsqrt(spread + 1e-05) * gain).astype(BF16)
        lp = jnp.dot(normed, wl4, preferred_element_type=F32)
        s_left[pl.ds(s, 256, stride=16), :] = lp
        rp = lax.dot_general(wrt, normed, NT, preferred_element_type=F32)
        s_right[0, pl.ds(s, 32, stride=16), :] = rp[:, :128]
        s_right[1, pl.ds(s, 32, stride=16), :] = rp[:, 128:]

    r_send[...] = s_right[1 - h].reshape(32, 16, 128).astype(BF16)

    pl.semaphore_wait(barrier, 31)

    my16 = pl.ds(pl.multiple_of(me * 16, 16), 16)
    sib_r = remote(r_send, r_all.at[:, my16, :], sib_send.at[0], sib_recv.at[0], sib)
    sib_r.start()
    sib_c = remote(
        coup.at[:, pl.ds(pl.multiple_of((1 - h) * 128, 128), 128), :],
        coup16.at[pl.ds(h * 8, 8)],
        sib_send.at[1],
        sib_recv.at[1],
        sib,
    )
    sib_c.start()
    r_all[:, my16, :] = s_right[h].reshape(32, 16, 128).astype(BF16)

    sib16 = pl.ds(pl.multiple_of(sib * 16, 16), 16)
    remote(r_send, r_all.at[:, sib16, :], sib_send.at[0], sib_recv.at[0], sib).wait_recv()

    def block(c, zz, xx, half=None):
        rows = pl.ds(pl.multiple_of((4 * zz + xx) * 32, 32), 32)
        if half is None:
            return r_all.at[pl.ds(c * ND, ND), rows, :]
        return r_all.at[pl.ds(c * ND + half * (ND // 2), ND // 2), rows, :]

    def z_copy(c, k):
        b = block(c, z, x)
        return remote(b, b, z_ssem.at[c, k], r_rsem.at[c, q], dev((z + k) % 4, x))

    def x_copy(c, zz, d):
        b = block(c, zz, x)
        return remote(
            b, b, x_ssem.at[c, zz, d // 2], r_rsem.at[c, 4 * zz + x], dev(z, (x + d) % 4)
        )

    def f_copy(c, zz, half):
        frm, to = ((x + 3) % 4, (x + 1) % 4) if half == 0 else ((x + 1) % 4, (x + 3) % 4)
        b = block(c, zz, frm, half)
        return remote(b, b, f_ssem.at[c, zz, half], f_rsem.at[c, zz, half], dev(z, to))

    def wait_block(c, zz, xx):
        b = block(c, zz, xx)
        remote(b, b, z_ssem.at[c, 0], r_rsem.at[c, 4 * zz + xx], sib).wait_recv()

    @pl.loop(0, CHUNKS)
    def _(c):
        for k in (1, 2, 3):
            z_copy(c, k).start()
        for d in (1, 3):
            x_copy(c, z, d).start()

    lane = lax.broadcasted_iota(jnp.int32, (4, 16, 128), 2)

    def l_copy(qq):
        return remote(
            l_send.at[qq], l_all.at[q, h], l_ssem.at[qq], l_rsem.at[q], 2 * qq + h
        )

    @pl.loop(0, 16)
    def _(k):
        qq = (q + k) % 16
        v = s_left[pl.ds(pl.multiple_of(qq * 256, 256), 256), :].reshape(4, 4, 16, 128)
        v = jnp.where(
            lane < 32,
            v[:, 0],
            jnp.where(lane < 64, v[:, 1], jnp.where(lane < 96, v[:, 2], v[:, 3])),
        ).astype(BF16)
        for g in range(4):
            l_send[qq, :, g * 128 : (g + 1) * 128] = v[g]

        @pl.when(k > 0)
        def _():
            l_copy(qq).start()

    l_all[q, h] = l_send[q]

    s_tri[0:1024, :] = w_final[...].astype(F32)
    for d in range(32):
        part = s_tri[pl.ds(d, 32, stride=32), :]
        s_tri[1024 + d * 32 : 1024 + (d + 1) * 32, :] = part
    for b in range(8):
        w2[:, b * 128 : (b + 1) * 128] = (
            s_tri[1024 + b * 128 : 1024 + (b + 1) * 128, :].T.astype(BF16)
        )
    for b, ref in enumerate((w_el, g_el, w_er, g_er, g_up)):
        w5[b * 128 : (b + 1) * 128, :] = ref[...].astype(F32).T.astype(BF16)
    wu[...] = w_up[...].astype(F32).T.astype(BF16)

    def l_wait(qq):
        remote(l_send.at[qq], l_all.at[qq, h], l_ssem.at[qq], l_rsem.at[qq], sib).wait_recv()

    def forward(c):
        for k in (1, 2, 3):
            zz = (z + k) % 4
            wait_block(c, zz, x)
            x_copy(c, zz, 1).start()
            x_copy(c, zz, 3).start()
        for k in range(4):
            zz = (z + k) % 4
            wait_block(c, zz, (x + 3) % 4)
            f_copy(c, zz, 0).start()
            wait_block(c, zz, (x + 1) % 4)
            f_copy(c, zz, 1).start()

    def finish(c):
        for k in range(4):
            zz = (z + k) % 4
            for half in (0, 1):
                b = block(c, zz, (x + 2) % 4, half)
                remote(
                    b, b, f_ssem.at[c, zz, half], f_rsem.at[c, zz, half], sib
                ).wait_recv()

        @pl.loop(0, ND // 2)
        def _(p):
            d = c * ND + 2 * p
            rhs = jnp.concatenate([r_all[d], r_all[d + 1]], axis=1)
            o = jnp.dot(l_t[...], rhs, preferred_element_type=F32) * (1.0 / 512)
            o = o.astype(BF16)
            outer[:, d] = o[:, :128].reshape(16, 32, 128)
            outer[:, d + 1] = o[:, 128:].reshape(16, 32, 128)

    forward(0)

    @pl.loop(1, 16)
    def _(k):
        l_wait((q + k) % 16)

    l_fwd = remote(l_all.at[:, h], l_all.at[:, h], sib_send.at[2], sib_recv.at[2], sib)
    l_fwd.start()
    remote(
        l_all.at[:, 1 - h], l_all.at[:, 1 - h], sib_send.at[2], sib_recv.at[2], sib
    ).wait_recv()
    for b in range(4):
        l_t[b * 128 : (b + 1) * 128, :] = (
            l_all[:, :, :, b * 128 : (b + 1) * 128].reshape(512, 128).astype(F32).T.astype(BF16)
        )

    coup16[pl.ds(h * 8, 8)] = coup[:, pl.ds(pl.multiple_of(h * 128, 128), 128), :]

    @pl.loop(1, CHUNKS)
    def _(c):
        forward(c)
        finish(c - 1)

    finish(CHUNKS - 1)

    remote(
        coup.at[:, pl.ds(0, 128), :],
        coup16.at[pl.ds((1 - h) * 8, 8)],
        sib_send.at[1],
        sib_recv.at[1],
        sib,
    ).wait_recv()
    eye = (
        lax.broadcasted_iota(jnp.int32, (128, 128), 0)
        == lax.broadcasted_iota(jnp.int32, (128, 128), 1)
    ).astype(F32).astype(BF16)
    p_gain = column(pair_gain[...])
    t_gain = column(tri_gain[...])

    @pl.loop(0, 8)
    def _(a):
        rhs = jnp.concatenate(
            [outer[2 * a].reshape(1024, 128), outer[2 * a + 1].reshape(1024, 128)], axis=1
        )
        u = jnp.dot(w2[...], rhs, preferred_element_type=F32)
        normed = []
        for e in (0, 1):
            i = 2 * a + e
            m = lax.dot_general(eye, coup16[i], NT, preferred_element_type=F32)
            m = m + u[:, e * 128 : (e + 1) * 128]
            mid[i] = m
            normed.append(norm_rows(m, p_gain))
        y = jnp.dot(w5[...], jnp.concatenate(normed, axis=1), preferred_element_type=F32)
        el = jax.nn.sigmoid(y[128:256]) * y[0:128]
        er = jax.nn.sigmoid(y[384:512]) * y[256:384]
        up = jax.nn.sigmoid(y[512:640])
        for e in (0, 1):
            i = 2 * a + e
            lanes = slice(e * 128, (e + 1) * 128)
            gate[i] = up[:, lanes]
            s_el[pl.ds(i, 128, stride=16), :] = el[:, lanes]
            s_er[pl.ds(i, 128, stride=16), :] = er[:, lanes]

    def e_copy(dst):
        return remote(e_send.at[dst], e_recv.at[me], e_ssem.at[dst], e_rsem.at[me], dst)

    @pl.loop(0, 32)
    def _(k):
        dst = (me + k) % 32
        rows = pl.ds(pl.multiple_of(dst * 64, 64), 64)
        e_send[dst, 0:4] = s_el[rows, :].reshape(4, 16, 128).astype(BF16)
        e_send[dst, 4:8] = s_er[rows, :].reshape(4, 16, 128).astype(BF16)

        @pl.when(k > 0)
        def _():
            e_copy(dst).start()

    e_recv[me] = e_send[me]

    @pl.loop(1, 32)
    def _(k):
        src = (me + k) % 32
        remote(e_send.at[src], e_recv.at[src], e_ssem.at[src], e_rsem.at[src], sib).wait_recv()

    for c in range(4):
        got = e_recv.reshape(16, 2, 8, 16, 128)
        t = None
        for hh in (0, 1):
            lhs = got[:, hh, c].reshape(256, 128)
            rhs = got[:, hh, 4 + c].reshape(256, 128)
            term = lax.dot_general(lhs, rhs, NT, preferred_element_type=F32)
            t = term if t is None else t + term
        t = t.astype(BF16)
        for hh in (0, 1):
            t_send[:, hh, c] = t[:, hh * 128 : (hh + 1) * 128].reshape(16, 16, 128)

    def t_copy(dst):
        return remote(
            t_send.at[dst // 2, dst % 2], t_recv.at[me], t_ssem.at[dst], t_rsem.at[me], dst
        )

    @pl.loop(1, 32)
    def _(k):
        t_copy((me + k) % 32).start()

    t_recv[me] = t_send[q, h]

    @pl.loop(1, 32)
    def _(k):
        src = (me + k) % 32
        remote(
            t_send.at[0, 0], t_recv.at[src], t_ssem.at[src], t_rsem.at[src], sib
        ).wait_recv()

    s_tri[...] = t_recv[...].reshape(2048, 128).astype(F32)

    def result(a):
        normed = [
            norm_rows(s_tri[pl.ds(2 * a + e, 128, stride=16), :], t_gain) for e in (0, 1)
        ]
        y = jnp.dot(wu[...], jnp.concatenate(normed, axis=1), preferred_element_type=F32)
        for e in (0, 1):
            i = 2 * a + e
            r = mid[i] + gate[i] * y[:, e * 128 : (e + 1) * 128]
            o_buf[i] = r.T.astype(BF16)

    @pl.loop(0, 4)
    def _(a):
        result(4 * (1 - h) + a)

    o_copy = remote(
        o_buf.at[pl.ds((1 - h) * 8, 8)], o_got, sib_send.at[3], sib_recv.at[3], sib
    )
    o_copy.start()

    @pl.loop(0, 4)
    def _(a):
        result(4 * h + a)

    out[:, pl.ds(pl.multiple_of(h * 128, 128), 128), :] = o_buf[pl.ds(h * 8, 8)]
    o_copy.wait_recv()
    out[:, pl.ds(pl.multiple_of((1 - h) * 128, 128), 128), :] = o_got[...]

    sib_r.wait_send()
    sib_c.wait_send()
    l_fwd.wait_send()
    o_copy.wait_send()

    @pl.loop(1, 16)
    def _(k):
        l_copy((q + k) % 16).wait_send()

    @pl.loop(0, CHUNKS)
    def _(c):
        for k in (1, 2, 3):
            z_copy(c, k).wait_send()
        for zz in range(4):
            x_copy(c, zz, 1).wait_send()
            x_copy(c, zz, 3).wait_send()
            f_copy(c, zz, 0).wait_send()
            f_copy(c, zz, 1).wait_send()

    @pl.loop(1, 32)
    def _(k):
        e_copy((me + k) % 32).wait_send()
        t_copy((me + k) % 32).wait_send()


def local(
    relative_embedding,
    coupling_features,
    relative_variance_multiplier,
    bilinear_lhs_projector,
    bilinear_rhs_projector,
    product_final_matrix,
    coupling_standard_scale,
    incoming_edge_matrix,
    incoming_edge_sigmoid,
    second_edge_matrix,
    second_edge_sigmoid,
    update_sigmoid_matrix,
    update_final_matrix,
    cubic_standard_scale,
):
    vm = pltpu.VMEM
    dma = pltpu.SemaphoreType.DMA
    return pl.pallas_call(
        kernel,
        out_shape=jax.ShapeDtypeStruct((8, 256, 128), BF16),
        in_specs=[pl.BlockSpec(memory_space=pltpu.VMEM)] * 14,
        out_specs=pl.BlockSpec(memory_space=pltpu.VMEM),
        scratch_shapes=[
            vm((4096, 128), F32),
            vm((2, 512, 128), F32),
            vm((16, 16, 512), BF16),
            vm((16, 2, 16, 512), BF16),
            vm((512, 512), BF16),
            vm((32, 16, 128), BF16),
            vm((32, 512, 128), BF16),
            vm((16, 32, 32, 128), BF16),
            vm((16, 128, 128), BF16),
            vm((128, 1024), BF16),
            vm((640, 128), BF16),
            vm((128, 128), BF16),
            vm((16, 128, 128), F32),
            vm((16, 128, 128), F32),
            vm((2048, 128), F32),
            vm((2048, 128), F32),
            vm((32, 8, 16, 128), BF16),
            vm((32, 8, 16, 128), BF16),
            vm((16, 2, 4, 16, 128), BF16),
            vm((32, 4, 16, 128), BF16),
            vm((2048, 128), F32),
            vm((16, 128, 128), BF16),
            vm((8, 128, 128), BF16),
            dma((4,)),
            dma((4,)),
            dma((16,)),
            dma((16,)),
            dma((CHUNKS, 4)),
            dma((CHUNKS, 4, 2)),
            dma((CHUNKS, 4, 2)),
            dma((CHUNKS, 16)),
            dma((CHUNKS, 4, 2)),
            dma((32,)),
            dma((32,)),
            dma((32,)),
            dma((32,)),
        ],
        compiler_params=pltpu.CompilerParams(
            collective_id=0, has_side_effects=True, vmem_limit_bytes=48 * 1024 * 1024
        ),
    )(
        relative_embedding,
        coupling_features,
        relative_variance_multiplier.reshape(1, -1),
        bilinear_lhs_projector,
        bilinear_rhs_projector,
        product_final_matrix,
        coupling_standard_scale.reshape(1, -1),
        incoming_edge_matrix,
        incoming_edge_sigmoid,
        second_edge_matrix,
        second_edge_sigmoid,
        update_sigmoid_matrix,
        update_final_matrix,
        cubic_standard_scale.reshape(1, -1),
    )


def solution(mesh):
    rows = P(("batch", "dap"), None, None)
    return jax.shard_map(
        local,
        mesh=mesh,
        in_specs=(rows, rows) + (P(),) * 12,
        out_specs=rows,
        check_vma=False,
    )
```

time: 266 us -> 136 us (0.51)
  the two profiles are of different devices: /device:TPU:1 before, /device:TPU:67 now
where the time goes in v1:
time: 136 us; the launch traced here: 135 us
  Pallas kernels  123 us (90%)
  local copies, waits for them, and re-layouts  12.6 us (9%)
    pallas_call x1, Pallas kernels, local(): pl.pallas_call(kernel, out_shape=jax.ShapeDtypeStruct((8, 256, 128), BF16...  123 us
    unnamed x27, local copies, waits for them, and re-layouts  12.6 us

profile of v1, /device:TPU:67, one launch (start us, length us, event | category | flops | bytes accessed | tf_op | source)
XLA Modules:
  0.0 135.3 jit_solution(14770219867804558946)
XLA Ops:
  0.0 0.8 copy.15.w_lhs
  0.8 0.8 copy.16.w_rhs
  1.7 0.0 copy-start
  1.7 1.6 %copy-done = bf16[16,256,256]{2,1,0:T(8,128)(2,1)S(1)} copy-done((bf16[16,256,256]{2,1,0:T(8,128)(2,1)S(1)}, bf16[16,256,256]{2,1,0:T(8,128)(2,1)}, u32[]{:S(2)}) %copy-start) | copy-done | bytes 2097176
  3.3 0.0 copy-start.1
  3.3 1.0 copy-done.1
  4.3 0.0 copy-start.2
  4.3 0.9 copy-done.2
  5.3 0.0 copy-start.3
  5.3 0.8 copy-done.3
  6.0 0.0 copy-start.4
  6.0 0.8 copy-done.4
  6.8 0.0 copy-start.5
  6.8 0.8 copy-done.5
  7.5 0.0 copy-start.6
  7.5 0.8 copy-done.6
  8.3 0.0 copy-start.7
  8.3 0.8 copy-done.7
  9.1 0.0 copy-start.8
  9.1 0.8 copy-done.8
  9.8 0.0 copy-start.9
  9.8 0.7 copy-done.9
  10.5 0.0 copy-start.10
  10.5 0.7 copy-done.10
  11.1 0.0 copy-start.11
  11.2 0.7 copy-done.11
  11.8 122.7 %shard_map.136 = bf16[8,256,128]{2,1,0:T(8,128)(2,1)S(1)} custom-call(bf16[16,256,256]{2,1,0:T(8,128)(2,1)S(1)} %copy-done, bf16[8,256,128]{2,1,0:T(8,128)(2,1)S(1)} %copy-done.1, f32[1,256]{1,0:T(1,128)S(1)} %bitcast.3, bf16[256,32]{1,0:T(8,128)(2,1)S(1)} %copy.15.w_lhs, bf16[256,32]{1,0:T(8,128)(2,1)S(1)} %copy.16.w_rhs, bf16[1024,128]{1,0:T(8,128)(2,1)S(1)} %copy-done.2, ...), custom_call_target="tpu_custom_call" | custom-call | tf_op jit(solution)/shard_map/pallas_call | solution.py:435
  134.5 0.8 copy.18
Async XLA Ops:
  1.7 1.6 %copy-start = (bf16[16,256,256]{2,1,0:T(8,128)(2,1)S(1)}, bf16[16,256,256]{2,1,0:T(8,128)(2,1)}, u32[]{:S(2)}) copy-start(bf16[16,256,256]{2,1,0:T(8,128)(2,1)} %msa.1) | copy-start | bytes 6291460
  3.3 1.0 copy-start.1
  4.3 0.9 copy-start.2
  5.3 0.8 copy-start.3
  6.0 0.8 copy-start.4
  6.8 0.8 copy-start.5
  7.5 0.8 copy-start.6
  8.3 0.8 copy-start.7
  9.1 0.8 copy-start.8
  9.8 0.7 copy-start.9
  10.5 0.7 copy-start.10
  11.1 0.7 copy-start.11

commit v2 on v1

--- a/solution.py
+++ b/solution.py
@@ -36,21 +36,28 @@
 
 
 def kernel(
+    msa_h,
+    coup_h,
+    msa_gain_h,
+    w_lhs_h,
+    w_rhs_h,
+    w_final_h,
+    pair_gain_h,
+    w_el_h,
+    g_el_h,
+    w_er_h,
+    g_er_h,
+    g_up_h,
+    w_up_h,
+    tri_gain_h,
+    out,
     msa,
-    coup,
     msa_gain,
     w_lhs,
     w_rhs,
     w_final,
-    pair_gain,
-    w_el,
-    g_el,
-    w_er,
-    g_er,
-    g_up,
-    w_up,
-    tri_gain,
-    out,
+    gains,
+    w_six,
     s_left,
     s_right,
     l_send,
@@ -74,6 +81,7 @@
     s_tri,
     o_buf,
     o_got,
+    in_sem,
     sib_send,
     sib_recv,
     l_ssem,
@@ -98,6 +106,31 @@
     def dev(zz, xx):
         return 2 * (4 * zz + xx) + h
 
+    def fetch(n, src, dst):
+        copy = pltpu.make_async_copy(src, dst, in_sem.at[n])
+        copy.start()
+        return copy
+
+    first = [
+        fetch(0, msa_gain_h, msa_gain),
+        fetch(1, w_lhs_h, w_lhs),
+        fetch(2, w_rhs_h, w_rhs),
+    ]
+    parts = [
+        fetch(3 + n, msa_h.at[pl.ds(4 * n, 4)], msa.at[pl.ds(4 * n, 4)]) for n in range(4)
+    ]
+    mine = pl.ds(pl.multiple_of(h * 128, 128), 128)
+    other = pl.ds(pl.multiple_of((1 - h) * 128, 128), 128)
+    later = [
+        fetch(7, w_final_h, w_final),
+        fetch(8, pair_gain_h, gains.at[0]),
+        fetch(9, tri_gain_h, gains.at[1]),
+        fetch(10, coup_h.at[:, mine, :], coup16.at[pl.ds(h * 8, 8)]),
+    ]
+    for n, ref in enumerate((w_el_h, g_el_h, w_er_h, g_er_h, g_up_h, w_up_h)):
+        later.append(fetch(11 + n, ref, w_six.at[n]))
+
+    pending = []
     barrier = pltpu.get_barrier_semaphore()
 
     @pl.loop(1, 32)
@@ -106,12 +139,13 @@
             barrier, inc=1, device_id={"dap": (me + k) % 32}, device_id_type=MESH
         )
 
-    wl4 = jnp.concatenate([w_lhs[...]] * 4, axis=1)
-    wrt = w_rhs[...].astype(F32).T.astype(BF16)
+    for copy in first:
+        copy.wait()
+    wl4 = jnp.concatenate([w_lhs[...].astype(F32)] * 4, axis=0).T.astype(BF16)
+    wrt = w_rhs[...]
     gain = msa_gain[...]
 
-    @pl.loop(0, 16)
-    def _(s):
+    def project(s):
         v = msa[s].astype(F32)
         mean = jnp.mean(v, axis=-1, keepdims=True)
         centred = v - mean
@@ -123,6 +157,10 @@
         s_right[0, pl.ds(s, 32, stride=16), :] = rp[:, :128]
         s_right[1, pl.ds(s, 32, stride=16), :] = rp[:, 128:]
 
+    for n in range(4):
+        parts[n].wait()
+        pl.loop(4 * n, 4 * n + 4)(project)
+
     r_send[...] = s_right[1 - h].reshape(32, 16, 128).astype(BF16)
 
     pl.semaphore_wait(barrier, 31)
@@ -131,13 +169,14 @@
     sib_r = remote(r_send, r_all.at[:, my16, :], sib_send.at[0], sib_recv.at[0], sib)
     sib_r.start()
     sib_c = remote(
-        coup.at[:, pl.ds(pl.multiple_of((1 - h) * 128, 128), 128), :],
+        coup_h.at[:, other, :],
         coup16.at[pl.ds(h * 8, 8)],
         sib_send.at[1],
         sib_recv.at[1],
         sib,
     )
     sib_c.start()
+    pending += [sib_r.wait_send, sib_c.wait_send]
     r_all[:, my16, :] = s_right[h].reshape(32, 16, 128).astype(BF16)
 
     sib16 = pl.ds(pl.multiple_of(sib * 16, 16), 16)
@@ -174,6 +213,18 @@
             z_copy(c, k).start()
         for d in (1, 3):
             x_copy(c, z, d).start()
+
+    def right_sent():
+        @pl.loop(0, CHUNKS)
+        def _(c):
+            for k in (1, 2, 3):
+                z_copy(c, k).wait_send()
+            for zz in range(4):
+                for n in (0, 1):
+                    x_copy(c, zz, 2 * n + 1).wait_send()
+                    f_copy(c, zz, n).wait_send()
+
+    pending.append(right_sent)
 
     lane = lax.broadcasted_iota(jnp.int32, (4, 16, 128), 2)
 
@@ -200,6 +251,15 @@
 
     l_all[q, h] = l_send[q]
 
+    def left_sent():
+        @pl.loop(1, 16)
+        def _(k):
+            l_copy((q + k) % 16).wait_send()
+
+    pending.append(left_sent)
+
+    for copy in later:
+        copy.wait()
     s_tri[0:1024, :] = w_final[...].astype(F32)
     for d in range(32):
         part = s_tri[pl.ds(d, 32, stride=32), :]
@@ -208,9 +268,9 @@
         w2[:, b * 128 : (b + 1) * 128] = (
             s_tri[1024 + b * 128 : 1024 + (b + 1) * 128, :].T.astype(BF16)
         )
-    for b, ref in enumerate((w_el, g_el, w_er, g_er, g_up)):
-        w5[b * 128 : (b + 1) * 128, :] = ref[...].astype(F32).T.astype(BF16)
-    wu[...] = w_up[...].astype(F32).T.astype(BF16)
+    for b in range(5):
+        w5[b * 128 : (b + 1) * 128, :] = w_six[b].astype(F32).T.astype(BF16)
+    wu[...] = w_six[5].astype(F32).T.astype(BF16)
 
     def l_wait(qq):
         remote(l_send.at[qq], l_all.at[qq, h], l_ssem.at[qq], l_rsem.at[qq], sib).wait_recv()
@@ -254,6 +314,7 @@
 
     l_fwd = remote(l_all.at[:, h], l_all.at[:, h], sib_send.at[2], sib_recv.at[2], sib)
     l_fwd.start()
+    pending.append(l_fwd.wait_send)
     remote(
         l_all.at[:, 1 - h], l_all.at[:, 1 - h], sib_send.at[2], sib_recv.at[2], sib
     ).wait_recv()
@@ -262,8 +323,6 @@
             l_all[:, :, :, b * 128 : (b + 1) * 128].reshape(512, 128).astype(F32).T.astype(BF16)
         )
 
-    coup16[pl.ds(h * 8, 8)] = coup[:, pl.ds(pl.multiple_of(h * 128, 128), 128), :]
-
     @pl.loop(1, CHUNKS)
     def _(c):
         forward(c)
@@ -272,7 +331,7 @@
     finish(CHUNKS - 1)
 
     remote(
-        coup.at[:, pl.ds(0, 128), :],
+        coup_h.at[:, other, :],
         coup16.at[pl.ds((1 - h) * 8, 8)],
         sib_send.at[1],
         sib_recv.at[1],
@@ -282,8 +341,8 @@
         lax.broadcasted_iota(jnp.int32, (128, 128), 0)
         == lax.broadcasted_iota(jnp.int32, (128, 128), 1)
     ).astype(F32).astype(BF16)
-    p_gain = column(pair_gain[...])
-    t_gain = column(tri_gain[...])
+    p_gain = column(gains[0])
+    t_gain = column(gains[1])
 
     @pl.loop(0, 8)
     def _(a):
@@ -323,6 +382,12 @@
         def _():
             e_copy(dst).start()
 
+    def edges_sent():
+        @pl.loop(1, 32)
+        def _(k):
+            e_copy((me + k) % 32).wait_send()
+
+    pending.append(edges_sent)
     e_recv[me] = e_send[me]
 
     @pl.loop(1, 32)
@@ -351,6 +416,12 @@
     def _(k):
         t_copy((me + k) % 32).start()
 
+    def tri_sent():
+        @pl.loop(1, 32)
+        def _(k):
+            t_copy((me + k) % 32).wait_send()
+
+    pending.append(tri_sent)
     t_recv[me] = t_send[q, h]
 
     @pl.loop(1, 32)
@@ -380,38 +451,18 @@
         o_buf.at[pl.ds((1 - h) * 8, 8)], o_got, sib_send.at[3], sib_recv.at[3], sib
     )
     o_copy.start()
+    pending.append(o_copy.wait_send)
 
     @pl.loop(0, 4)
     def _(a):
         result(4 * h + a)
 
-    out[:, pl.ds(pl.multiple_of(h * 128, 128), 128), :] = o_buf[pl.ds(h * 8, 8)]
+    out[:, mine, :] = o_buf[pl.ds(h * 8, 8)]
     o_copy.wait_recv()
-    out[:, pl.ds(pl.multiple_of((1 - h) * 128, 128), 128), :] = o_got[...]
-
-    sib_r.wait_send()
-    sib_c.wait_send()
-    l_fwd.wait_send()
-    o_copy.wait_send()
-
-    @pl.loop(1, 16)
-    def _(k):
-        l_copy((q + k) % 16).wait_send()
-
-    @pl.loop(0, CHUNKS)
-    def _(c):
-        for k in (1, 2, 3):
-            z_copy(c, k).wait_send()
-        for zz in range(4):
-            x_copy(c, zz, 1).wait_send()
-            x_copy(c, zz, 3).wait_send()
-            f_copy(c, zz, 0).wait_send()
-            f_copy(c, zz, 1).wait_send()
-
-    @pl.loop(1, 32)
-    def _(k):
-        e_copy((me + k) % 32).wait_send()
-        t_copy((me + k) % 32).wait_send()
+    out[:, other, :] = o_got[...]
+
+    for wait in pending:
+        wait()
 
 
 def local(
@@ -435,9 +486,16 @@
     return pl.pallas_call(
         kernel,
         out_shape=jax.ShapeDtypeStruct((8, 256, 128), BF16),
-        in_specs=[pl.BlockSpec(memory_space=pltpu.VMEM)] * 14,
+        in_specs=[pl.BlockSpec(memory_space=pl.ANY)] * 14,
         out_specs=pl.BlockSpec(memory_space=pltpu.VMEM),
         scratch_shapes=[
+            vm((16, 256, 256), BF16),
+            vm((1, 256), F32),
+            vm((32, 256), BF16),
+            vm((32, 256), BF16),
+            vm((1024, 128), BF16),
+            vm((2, 1, 128), F32),
+            vm((6, 128, 128), BF16),
             vm((4096, 128), F32),
             vm((2, 512, 128), F32),
             vm((16, 16, 512), BF16),
@@ -461,6 +519,7 @@
             vm((2048, 128), F32),
             vm((16, 128, 128), BF16),
             vm((8, 128, 128), BF16),
+            dma((17,)),
             dma((4,)),
             dma((4,)),
             dma((16,)),
@@ -482,8 +541,8 @@
         relative_embedding,
         coupling_features,
         relative_variance_multiplier.reshape(1, -1),
-        bilinear_lhs_projector,
-        bilinear_rhs_projector,
+        bilinear_lhs_projector.T,
+        bilinear_rhs_projector.T,
         product_final_matrix,
         coupling_standard_scale.reshape(1, -1),
         incoming_edge_matrix,

time: 136 us -> 137 us (level)
  the two profiles are of different devices: /device:TPU:67 before, /device:TPU:75 now
where the time goes in v2:
time: 137 us; the launch traced here: 136 us
  Pallas kernels  124 us (91%)
  local copies, waits for them, and re-layouts  12.3 us (9%)
    pallas_call x1, Pallas kernels, local(): pl.pallas_call(kernel, out_shape=jax.ShapeDtypeStruct((8, 256, 128), BF16...  124 us
    unnamed x29, local copies, waits for them, and re-layouts  12.3 us

profile of v2, /device:TPU:75, one launch (start us, length us, event | category | flops | bytes accessed | tf_op | source)
XLA Modules:
  0.0 136.2 jit_solution(6467440380410379404)
XLA Ops:
  0.0 0.0 copy-start
  0.0 1.6 %copy-done = bf16[16,256,256]{2,1,0:T(8,128)(2,1)S(1)} copy-done((bf16[16,256,256]{2,1,0:T(8,128)(2,1)S(1)}, bf16[16,256,256]{2,1,0:T(8,128)(2,1)}, u32[]{:S(2)}) %copy-start) | copy-done | bytes 2097176
  1.6 0.0 copy-start.1
  1.6 1.0 copy-done.1
  2.6 0.0 copy-start.2
  2.6 0.9 copy-done.2
  3.6 0.0 copy-start.3
  3.6 0.8 copy-done.3
  4.3 0.0 copy-start.4
  4.3 0.8 copy-done.4
  5.1 0.0 copy-start.5
  5.1 0.8 copy-done.5
  5.9 0.0 copy-start.6
  5.9 0.8 copy-done.6
  6.6 0.0 copy-start.7
  6.6 0.8 copy-done.7
  7.4 0.0 copy-start.8
  7.4 0.8 copy-done.8
  8.1 0.0 copy-start.9
  8.1 0.7 copy-done.9
  8.9 0.0 copy-start.10
  8.9 0.7 copy-done.10
  9.6 0.0 copy-start.11
  9.6 0.7 copy-done.11
  10.3 0.0 copy-start.12
  10.3 0.7 copy-done.12
  10.9 0.0 copy-start.13
  10.9 0.7 copy-done.13
  11.6 123.8 %shard_map.136 = bf16[8,256,128]{2,1,0:T(8,128)(2,1)S(1)} custom-call(bf16[16,256,256]{2,1,0:T(8,128)(2,1)S(1)} %copy-done, bf16[8,256,128]{2,1,0:T(8,128)(2,1)S(1)} %copy-done.1, f32[1,256]{1,0:T(1,128)S(1)} %bitcast.7, bf16[32,256]{1,0:T(8,128)(2,1)S(1)} %bitcast.5, bf16[32,256]{1,0:T(8,128)(2,1)S(1)} %bitcast.6, bf16[1024,128]{1,0:T(8,128)(2,1)S(1)} %copy-done.2, ...), custom_call_target="tpu_custom_call" | custom-call | tf_op jit(solution)/shard_map/pallas_call | solution.py:486
  135.4 0.8 copy.16
Async XLA Ops:
  0.0 1.6 %copy-start = (bf16[16,256,256]{2,1,0:T(8,128)(2,1)S(1)}, bf16[16,256,256]{2,1,0:T(8,128)(2,1)}, u32[]{:S(2)}) copy-start(bf16[16,256,256]{2,1,0:T(8,128)(2,1)} %msa_h.1) | copy-start | bytes 6291460
  1.6 1.0 copy-start.1
  2.6 0.9 copy-start.2
  3.6 0.8 copy-start.3
  4.3 0.8 copy-start.4
  5.1 0.8 copy-start.5
  5.9 0.8 copy-start.6
  6.6 0.8 copy-start.7
  7.4 0.8 copy-start.8
  8.1 0.7 copy-start.9
  8.9 0.7 copy-start.10
  9.6 0.7 copy-start.11
  10.3 0.7 copy-start.12
  10.9 0.7 copy-start.13

commit v3 on v2

--- a/solution.py
+++ b/solution.py
@@ -8,7 +8,7 @@
 MESH = pl.DeviceIdType.MESH
 F32 = jnp.float32
 BF16 = jnp.bfloat16
-CHUNKS = 4
+CHUNKS = 8
 ND = 32 // CHUNKS
 NT = (((1,), (1,)), ((), ()))
 
@@ -207,12 +207,14 @@
         b = block(c, zz, xx)
         remote(b, b, z_ssem.at[c, 0], r_rsem.at[c, 4 * zz + xx], sib).wait_recv()
 
-    @pl.loop(0, CHUNKS)
-    def _(c):
+    def start(c):
         for k in (1, 2, 3):
             z_copy(c, k).start()
         for d in (1, 3):
             x_copy(c, z, d).start()
+
+    start(0)
+    start(1)
 
     def right_sent():
         @pl.loop(0, CHUNKS)
@@ -275,12 +277,16 @@
     def l_wait(qq):
         remote(l_send.at[qq], l_all.at[qq, h], l_ssem.at[qq], l_rsem.at[qq], sib).wait_recv()
 
-    def forward(c):
+    def spread(c, more=True):
         for k in (1, 2, 3):
             zz = (z + k) % 4
             wait_block(c, zz, x)
             x_copy(c, zz, 1).start()
             x_copy(c, zz, 3).start()
+        if more:
+            start(c + 2)
+
+    def forward(c):
         for k in range(4):
             zz = (z + k) % 4
             wait_block(c, zz, (x + 3) % 4)
@@ -306,6 +312,8 @@
             outer[:, d] = o[:, :128].reshape(16, 32, 128)
             outer[:, d + 1] = o[:, 128:].reshape(16, 32, 128)
 
+    spread(0)
+    spread(1)
     forward(0)
 
     @pl.loop(1, 16)
@@ -323,11 +331,18 @@
             l_all[:, :, :, b * 128 : (b + 1) * 128].reshape(512, 128).astype(F32).T.astype(BF16)
         )
 
-    @pl.loop(1, CHUNKS)
+    @pl.loop(2, CHUNKS - 2)
     def _(c):
-        forward(c)
-        finish(c - 1)
-
+        spread(c)
+        forward(c - 1)
+        finish(c - 2)
+
+    for c in (CHUNKS - 2, CHUNKS - 1):
+        spread(c, False)
+        forward(c - 1)
+        finish(c - 2)
+    forward(CHUNKS - 1)
+    finish(CHUNKS - 2)
     finish(CHUNKS - 1)
 
     remote(
@@ -368,68 +383,117 @@
             s_el[pl.ds(i, 128, stride=16), :] = el[:, lanes]
             s_er[pl.ds(i, 128, stride=16), :] = er[:, lanes]
 
-    def e_copy(dst):
-        return remote(e_send.at[dst], e_recv.at[me], e_ssem.at[dst], e_rsem.at[me], dst)
-
-    @pl.loop(0, 32)
-    def _(k):
-        dst = (me + k) % 32
-        rows = pl.ds(pl.multiple_of(dst * 64, 64), 64)
-        e_send[dst, 0:4] = s_el[rows, :].reshape(4, 16, 128).astype(BF16)
-        e_send[dst, 4:8] = s_er[rows, :].reshape(4, 16, 128).astype(BF16)
-
-        @pl.when(k > 0)
-        def _():
-            e_copy(dst).start()
+    zh = me // 16
+    m_own = me % 16
+
+    def e_near(g, m):
+        return remote(
+            e_send.at[m, g], e_recv.at[me, g], e_ssem.at[g, m], e_rsem.at[g, me], zh * 16 + m
+        )
+
+    def e_far(g, m):
+        return remote(
+            e_send.at[m, g, pl.ds(4, 4)],
+            e_recv.at[me, g, pl.ds(4, 4)],
+            e_ssem.at[g, 16 + m],
+            e_rsem.at[g, me],
+            (1 - zh) * 16 + m,
+        )
+
+    for g in (0, 1):
+
+        @pl.loop(0, 16)
+        def _(k):
+            m = (m_own + k) % 16
+            rows = pl.ds(pl.multiple_of(m * 128 + g * 64, 64), 64)
+            e_send[m, g, 0:4] = s_el[rows, :].reshape(4, 16, 128).astype(BF16)
+            e_send[m, g, 4:8] = s_er[rows, :].reshape(4, 16, 128).astype(BF16)
+            e_far(g, m).start()
+
+            @pl.when(k > 0)
+            def _():
+                e_near(g, m).start()
+
+        e_recv[me, g] = e_send[m_own, g]
 
     def edges_sent():
-        @pl.loop(1, 32)
+        for g in (0, 1):
+
+            @pl.loop(0, 16)
+            def _(k):
+                m = (m_own + k) % 16
+                e_far(g, m).wait_send()
+
+                @pl.when(k > 0)
+                def _():
+                    e_near(g, m).wait_send()
+
+    pending.append(edges_sent)
+
+    def t_copy(g, m):
+        return remote(
+            t_send.at[m // 2, m % 2, g],
+            t_recv.at[m_own, g],
+            t_ssem.at[g, m],
+            t_rsem.at[g, m_own],
+            zh * 16 + m,
+        )
+
+    got = e_recv.reshape(2, 8, 2, 2, 8, 16, 128)
+    for g in (0, 1):
+
+        @pl.loop(0, 16)
         def _(k):
-            e_copy((me + k) % 32).wait_send()
-
-    pending.append(edges_sent)
-    e_recv[me] = e_send[me]
-
-    @pl.loop(1, 32)
-    def _(k):
-        src = (me + k) % 32
-        remote(e_send.at[src], e_recv.at[src], e_ssem.at[src], e_rsem.at[src], sib).wait_recv()
-
-    for c in range(4):
-        got = e_recv.reshape(16, 2, 8, 16, 128)
-        t = None
-        for hh in (0, 1):
-            lhs = got[:, hh, c].reshape(256, 128)
-            rhs = got[:, hh, 4 + c].reshape(256, 128)
-            term = lax.dot_general(lhs, rhs, NT, preferred_element_type=F32)
-            t = term if t is None else t + term
-        t = t.astype(BF16)
-        for hh in (0, 1):
-            t_send[:, hh, c] = t[:, hh * 128 : (hh + 1) * 128].reshape(16, 16, 128)
-
-    def t_copy(dst):
-        return remote(
-            t_send.at[dst // 2, dst % 2], t_recv.at[me], t_ssem.at[dst], t_rsem.at[me], dst
-        )
-
-    @pl.loop(1, 32)
-    def _(k):
-        t_copy((me + k) % 32).start()
+            m = (m_own + k) % 16
+            far = (1 - zh) * 16 + m
+            near = zh * 16 + m
+            remote(
+                e_send.at[m, g, pl.ds(4, 4)],
+                e_recv.at[far, g, pl.ds(4, 4)],
+                e_ssem.at[g, m],
+                e_rsem.at[g, far],
+                sib,
+            ).wait_recv()
+
+            @pl.when(k > 0)
+            def _():
+                remote(
+                    e_send.at[m, g], e_recv.at[near, g], e_ssem.at[g, m], e_rsem.at[g, near], sib
+                ).wait_recv()
+
+        for c in range(4):
+            t = None
+            for hh in (0, 1):
+                lhs = got[zh, :, hh, g, c].reshape(128, 128)
+                rhs = got[:, :, hh, g, 4 + c].reshape(256, 128)
+                term = lax.dot_general(lhs, rhs, NT, preferred_element_type=F32)
+                t = term if t is None else t + term
+            t = t.astype(BF16)
+            for hh in (0, 1):
+                t_send[:, hh, g, c] = t[:, hh * 128 : (hh + 1) * 128].reshape(8, 16, 128)
+
+        @pl.loop(1, 16)
+        def _(k):
+            t_copy(g, (m_own + k) % 16).start()
+
+        t_recv[m_own, g] = t_send[m_own // 2, h, g]
 
     def tri_sent():
-        @pl.loop(1, 32)
+        for g in (0, 1):
+
+            @pl.loop(1, 16)
+            def _(k):
+                t_copy(g, (m_own + k) % 16).wait_send()
+
+    pending.append(tri_sent)
+    for g in (0, 1):
+
+        @pl.loop(1, 16)
         def _(k):
-            t_copy((me + k) % 32).wait_send()
-
-    pending.append(tri_sent)
-    t_recv[me] = t_send[q, h]
-
-    @pl.loop(1, 32)
-    def _(k):
-        src = (me + k) % 32
-        remote(
-            t_send.at[0, 0], t_recv.at[src], t_ssem.at[src], t_rsem.at[src], sib
-        ).wait_recv()
+            m = (m_own + k) % 16
+            remote(
+                t_send.at[0, 0, g], t_recv.at[m, g], t_ssem.at[g, m], t_rsem.at[g, m], sib
+            ).wait_recv()
 
     s_tri[...] = t_recv[...].reshape(2048, 128).astype(F32)
 
@@ -512,10 +576,10 @@
             vm((16, 128, 128), F32),
             vm((2048, 128), F32),
             vm((2048, 128), F32),
-            vm((32, 8, 16, 128), BF16),
-            vm((32, 8, 16, 128), BF16),
+            vm((16, 2, 8, 16, 128), BF16),
+            vm((32, 2, 8, 16, 128), BF16),
+            vm((8, 2, 2, 4, 16, 128), BF16),
             vm((16, 2, 4, 16, 128), BF16),
-            vm((32, 4, 16, 128), BF16),
             vm((2048, 128), F32),
             vm((16, 128, 128), BF16),
             vm((8, 128, 128), BF16),
@@ -529,13 +593,13 @@
             dma((CHUNKS, 4, 2)),
             dma((CHUNKS, 16)),
             dma((CHUNKS, 4, 2)),
-            dma((32,)),
-            dma((32,)),
-            dma((32,)),
-            dma((32,)),
+            dma((2, 32)),
+            dma((2, 32)),
+            dma((2, 16)),
+            dma((2, 16)),
         ],
         compiler_params=pltpu.CompilerParams(
-            collective_id=0, has_side_effects=True, vmem_limit_bytes=48 * 1024 * 1024
+            collective_id=0, has_side_effects=True, vmem_limit_bytes=60 * 1024 * 1024
         ),
     )(
         relative_embedding,

time: 137 us -> 108 us (0.79)
  the two profiles are of different devices: /device:TPU:75 before, /device:TPU:1 now
where the time goes in v3:
time: 108 us
  Pallas kernels  106 us (98%)
  local copies, waits for them, and re-layouts  1.87 us (2%)
    pallas_call x1, Pallas kernels, local(): pl.pallas_call(kernel, out_shape=jax.ShapeDtypeStruct((8, 256, 128), BF16...  106 us

profile of v3, /device:TPU:1, one launch (start us, length us, event | category | flops | bytes accessed | tf_op | source)
XLA Modules:
  0.0 108.0 jit_solution(11211301871285554611)
XLA Ops:
  0.0 106.1 %shard_map.136 = bf16[8,256,128]{2,1,0:T(8,128)(2,1)} custom-call(bf16[16,256,256]{2,1,0:T(8,128)(2,1)} %msa_h.1, bf16[8,256,128]{2,1,0:T(8,128)(2,1)} %coup_h.1, f32[1,256]{1,0:T(1,128)} %bitcast.7, bf16[32,256]{1,0:T(8,128)(2,1)} %bitcast.5, bf16[32,256]{1,0:T(8,128)(2,1)} %bitcast.6, bf16[1024,128]{1,0:T(8,128)(2,1)} %w_final_h.1, f32[1,128]{1,0:T(1,128)} %bitcast.8, ...), custom_call_target="tpu_custom_call" | custom-call | tf_op jit(solution)/shard_map/pallas_call | solution.py:550
  106.1 1.9 %copy.16 = bf16[8,256,128]{2,1,0:T(8,128)(2,1)} copy(bf16[8,256,128]{2,1,0:T(8,128)(2,1)} %shard_map.136) | data formatting | bytes 1048576

commit v4 on v3

v4 whole, which is shorter than its diff:
```python
import jax
import jax.numpy as jnp
from jax import lax
from jax.experimental import pallas as pl
from jax.experimental.pallas import tpu as pltpu
from jax.sharding import PartitionSpec as P

MESH = pl.DeviceIdType.MESH
F32 = jnp.float32
BF16 = jnp.bfloat16
CHUNKS = 8
ND = 32 // CHUNKS
NT = (((1,), (1,)), ((), ()))


def remote(src, dst, send_sem, recv_sem, target):
    return pltpu.make_async_remote_copy(
        src_ref=src,
        dst_ref=dst,
        send_sem=send_sem,
        recv_sem=recv_sem,
        device_id={"dap": target},
        device_id_type=MESH,
    )


def column(row):
    return jnp.broadcast_to(row, (128, 128)).T


def norm_rows(v, gain):
    mean = jnp.mean(v, axis=0, keepdims=True)
    centred = v - mean
    spread = jnp.mean(centred * centred, axis=0, keepdims=True)
    return (centred * lax.rsqrt(spread + 1e-05) * gain).astype(BF16)


def kernel(
    msa_h,
    coup_h,
    msa_gain_h,
    w_lhs_h,
    w_rhs_h,
    w_final_h,
    pair_gain_h,
    w_el_h,
    g_el_h,
    w_er_h,
    g_er_h,
    g_up_h,
    w_up_h,
    tri_gain_h,
    out,
    msa,
    msa_gain,
    w_lhs,
    w_rhs,
    w_final,
    gains,
    w_six,
    s_left,
    s_right,
    l_send,
    l_all,
    l_t,
    r_send,
    r_all,
    outer,
    coup16,
    w2,
    w5,
    wu,
    mid,
    gate,
    normed,
    s_el,
    s_er,
    e_send,
    e_recv,
    t_send,
    t_recv,
    s_tri,
    o_buf,
    o_got,
    in_sem,
    sib_send,
    sib_recv,
    l_ssem,
    l_rsem,
    z_ssem,
    x_ssem,
    f_ssem,
    z_rsem,
    x_rsem,
    f_rsem,
    e_ssem,
    e_rsem,
    t_ssem,
    t_rsem,
):
    me = lax.axis_index("dap")
    h = me % 2
    q = me // 2
    x = q % 4
    z = q // 4
    sib = 2 * q + (1 - h)
    pos = 4 * x + z

    def dev(zz, xx):
        return 2 * (4 * zz + xx) + h

    def fetch(n, src, dst):
        copy = pltpu.make_async_copy(src, dst, in_sem.at[n])
        copy.start()
        return copy

    first = [
        fetch(0, msa_gain_h, msa_gain),
        fetch(1, w_lhs_h, w_lhs),
        fetch(2, w_rhs_h, w_rhs),
    ]
    parts = [
        fetch(3 + n, msa_h.at[pl.ds(4 * n, 4)], msa.at[pl.ds(4 * n, 4)]) for n in range(4)
    ]
    mine = pl.ds(pl.multiple_of(h * 128, 128), 128)
    other = pl.ds(pl.multiple_of((1 - h) * 128, 128), 128)
    later = [
        fetch(7, w_final_h, w_final),
        fetch(8, pair_gain_h, gains.at[0]),
        fetch(9, tri_gain_h, gains.at[1]),
        fetch(10, coup_h.at[:, mine, :], coup16.at[pl.ds(h * 8, 8)]),
    ]
    for n, ref in enumerate((w_el_h, g_el_h, w_er_h, g_er_h, g_up_h, w_up_h)):
        fetch(11, ref, w_six.at[n])
    later.append(pltpu.make_async_copy(w_six, w_six, in_sem.at[11]))

    pending = []
    barrier = pltpu.get_barrier_semaphore()

    @pl.loop(1, 32)
    def _(k):
        pl.semaphore_signal(
            barrier, inc=1, device_id={"dap": (me + k) % 32}, device_id_type=MESH
        )

    for copy in first:
        copy.wait()
    wl4 = jnp.concatenate([w_lhs[...].astype(F32)] * 4, axis=0).T.astype(BF16)
    wrt = w_rhs[...]
    gain = msa_gain[...]

    def project(s):
        v = msa[s].astype(F32)
        mean = jnp.mean(v, axis=-1, keepdims=True)
        centred = v - mean
        spread = jnp.mean(centred * centred, axis=-1, keepdims=True)
        normed = (centred * lax.rsqrt(spread + 1e-05) * gain).astype(BF16)
        lp = jnp.dot(normed, wl4, preferred_element_type=F32)
        s_left[pl.ds(s, 256, stride=16), :] = lp
        rp = lax.dot_general(wrt, normed, NT, preferred_element_type=F32)
        s_right[0, pl.ds(s, 32, stride=16), :] = rp[:, :128]
        s_right[1, pl.ds(s, 32, stride=16), :] = rp[:, 128:]

    for n in range(4):
        parts[n].wait()
        pl.loop(4 * n, 4 * n + 4)(project)

    r_send[...] = s_right[1 - h].reshape(32, 16, 128).astype(BF16)

    pl.semaphore_wait(barrier, 31)

    my16 = pl.ds(pl.multiple_of((2 * pos + h) * 16, 16), 16)
    sib_r = remote(r_send, r_all.at[:, my16, :], sib_send.at[0], sib_recv.at[0], sib)
    sib_r.start()
    sib_c = remote(
        coup_h.at[:, other, :],
        coup16.at[pl.ds(h * 8, 8)],
        sib_send.at[1],
        sib_recv.at[1],
        sib,
    )
    sib_c.start()
    pending += [sib_r.wait_send, sib_c.wait_send]
    r_all[:, my16, :] = s_right[h].reshape(32, 16, 128).astype(BF16)

    sib16 = pl.ds(pl.multiple_of((2 * pos + 1 - h) * 16, 16), 16)
    remote(r_send, r_all.at[:, sib16, :], sib_send.at[0], sib_recv.at[0], sib).wait_recv()

    def block(c, zz, xx):
        rows = pl.ds(pl.multiple_of((4 * xx + zz) * 32, 32), 32)
        return r_all.at[pl.ds(c * ND, ND), rows, :]

    def blocks(c, xx, half=None):
        rows = pl.ds(pl.multiple_of(xx * 128, 128), 128)
        if half is None:
            return r_all.at[pl.ds(c * ND, ND), rows, :]
        return r_all.at[pl.ds(c * ND + half * (ND // 2), ND // 2), rows, :]

    def z_copy(c, k):
        b = block(c, z, x)
        return remote(b, b, z_ssem, z_rsem.at[c], dev((z + k) % 4, x))

    def x_copy(c, zz, n):
        b = block(c, zz, x)
        return remote(b, b, x_ssem, x_rsem.at[c, n], dev(z, (x + 1 + 2 * n) % 4))

    def f_copy(c, n):
        b = blocks(c, (x + 3 - 2 * n) % 4, n)
        return remote(b, b, f_ssem, f_rsem.at[c, n], dev(z, (x + 1 + 2 * n) % 4))

    def z_wait(c):
        three = r_all.at[pl.ds(c * ND, ND), pl.ds(0, 96), :]
        remote(three, three, z_ssem, z_rsem.at[c], sib).wait_recv()

    def x_wait(c, n):
        b = blocks(c, (x + 3 - 2 * n) % 4)
        remote(b, b, x_ssem, x_rsem.at[c, n], sib).wait_recv()

    def f_wait(c, n):
        b = blocks(c, (x + 2) % 4, n)
        remote(b, b, f_ssem, f_rsem.at[c, n], sib).wait_recv()

    def z_start(c):
        for k in (1, 2, 3):
            z_copy(c, k).start()

    def sent(ref, sem):
        pending.append(remote(ref, ref, sem, sib_recv.at[0], sib).wait_send)

    z_start(0)

    @pl.loop(0, CHUNKS)
    def _(c):
        for n in (0, 1):
            x_copy(c, z, n).start()

    z_start(1)
    sent(r_all.at[pl.ds(0, 3 * CHUNKS), pl.ds(0, 32 * ND), :], z_ssem)
    sent(r_all.at[pl.ds(0, 16)], x_ssem)
    sent(r_all.at[pl.ds(0, 8)], f_ssem)

    lane = lax.broadcasted_iota(jnp.int32, (4, 16, 128), 2)

    def l_copy(qq):
        return remote(
            l_send.at[qq], l_all.at[pos, h], l_ssem, l_rsem, 2 * qq + h
        )

    @pl.loop(0, 16)
    def _(k):
        qq = (q + k) % 16
        v = s_left[pl.ds(pl.multiple_of(qq * 256, 256), 256), :].reshape(4, 4, 16, 128)
        v = jnp.where(
            lane < 32,
            v[:, 0],
            jnp.where(lane < 64, v[:, 1], jnp.where(lane < 96, v[:, 2], v[:, 3])),
        ).astype(BF16)
        for g in range(4):
            l_send[qq, :, g * 128 : (g + 1) * 128] = v[g]

        @pl.when(k > 0)
        def _():
            l_copy(qq).start()

    l_all[pos, h] = l_send[q]

    sent(l_all.at[pl.ds(0, 15), 0], l_ssem)

    def spread(c):
        z_wait(c)
        for k in (1, 2, 3):
            for n in (0, 1):
                x_copy(c, (z + k) % 4, n).start()
        if c + 2 < CHUNKS:
            z_start(c + 2)

    def forward(c):
        for n in (0, 1):
            x_wait(c, n)
            f_copy(c, n).start()

    def finish(c):
        for n in (0, 1):
            f_wait(c, n)

        for p in range(ND // 2):
            d = c * ND + 2 * p
            rhs = jnp.concatenate([r_all[d], r_all[d + 1]], axis=1)
            o = jnp.dot(l_t[...], rhs, preferred_element_type=F32) * (1.0 / 512)
            o = o.astype(BF16)
            outer[:, 2 * p] = o[:, :128].reshape(16, 32, 128)
            outer[:, 2 * p + 1] = o[:, 128:].reshape(16, 32, 128)

        @pl.loop(0, 8)
        def _(a):
            rhs = jnp.concatenate(
                [outer[2 * a].reshape(128, 128), outer[2 * a + 1].reshape(128, 128)], axis=1
            )
            u = jnp.dot(w2[c], rhs, preferred_element_type=F32)
            mid[2 * a] += u[:, :128]
            mid[2 * a + 1] += u[:, 128:]

    spread(0)
    spread(1)

    for copy in later:
        copy.wait()
    s_tri[0:1024, :] = w_final[...].astype(F32)
    for d in range(32):
        part = s_tri[pl.ds(d, 32, stride=32), :]
        s_tri[1024 + d * 32 : 1024 + (d + 1) * 32, :] = part
    for b in range(8):
        w2[b] = s_tri[1024 + b * 128 : 1024 + (b + 1) * 128, :].T.astype(BF16)
    for b in range(4):
        t = w_six[b].astype(F32).T.astype(BF16)
        w5[0, b * 64 : (b + 1) * 64, :] = t[:64]
        w5[1, b * 64 : (b + 1) * 64, :] = t[64:]
    for b in range(2):
        wu[b] = w_six[4 + b].astype(F32).T.astype(BF16)
    p_gain = column(gains[0])
    t_gain = column(gains[1])

    spread(2)
    forward(0)

    remote(
        coup_h.at[:, other, :],
        coup16.at[pl.ds((1 - h) * 8, 8)],
        sib_send.at[1],
        sib_recv.at[1],
        sib,
    ).wait_recv()
    eye = (
        lax.broadcasted_iota(jnp.int32, (128, 128), 0)
        == lax.broadcasted_iota(jnp.int32, (128, 128), 1)
    ).astype(F32).astype(BF16)

    @pl.loop(0, 16)
    def _(i):
        mid[i] = lax.dot_general(eye, coup16[i], NT, preferred_element_type=F32)

    forward(1)
    remote(
        l_all.at[pl.ds(0, 15), h], l_all.at[pl.ds(0, 15), h], l_ssem, l_rsem, sib
    ).wait_recv()
    l_fwd = remote(l_all.at[:, h], l_all.at[:, h], sib_send.at[2], sib_recv.at[2], sib)
    l_fwd.start()
    pending.append(l_fwd.wait_send)
    spread(3)
    remote(
        l_all.at[:, 1 - h], l_all.at[:, 1 - h], sib_send.at[2], sib_recv.at[2], sib
    ).wait_recv()
    for b in range(4):
        l_t[b * 128 : (b + 1) * 128, :] = (
            l_all[:, :, :, b * 128 : (b + 1) * 128].reshape(512, 128).astype(F32).T.astype(BF16)
        )

    finish(0)
    forward(2)
    finish(1)
    for c in range(4, CHUNKS):
        spread(c)
        forward(c - 1)
        finish(c - 2)
    forward(CHUNKS - 1)
    finish(CHUNKS - 2)
    finish(CHUNKS - 1)


    zh = me // 16
    m_own = me % 16

    def e_near(g, m):
        return remote(e_send.at[m, g], e_recv.at[me, g], e_ssem, e_rsem.at[g], zh * 16 + m)

    def e_far(g, m):
        four = pl.ds(4, 4)
        return remote(
            e_send.at[m, g, four],
            e_recv.at[me, g, four],
            e_ssem,
            e_rsem.at[g],
            (1 - zh) * 16 + m,
        )

    def edges(g, a):
        y = jnp.dot(w5[g], normed[a], preferred_element_type=F32)
        el = jax.nn.sigmoid(y[64:128]) * y[0:64]
        er = jax.nn.sigmoid(y[192:256]) * y[128:192]
        for e in (0, 1):
            rows = pl.ds(2 * a + e, 64, stride=16)
            s_el[rows, :] = el[:, e * 128 : (e + 1) * 128]
            s_er[rows, :] = er[:, e * 128 : (e + 1) * 128]

    def edges_send(g):
        @pl.loop(0, 16)
        def _(k):
            m = (m_own + k) % 16
            rows = pl.ds(pl.multiple_of(m * 64, 64), 64)
            e_send[m, g, 0:4] = s_el[rows, :].reshape(4, 16, 128).astype(BF16)
            e_send[m, g, 4:8] = s_er[rows, :].reshape(4, 16, 128).astype(BF16)
            e_far(g, m).start()

            @pl.when(k > 0)
            def _():
                e_near(g, m).start()

        e_recv[me, g] = e_send[m_own, g]

    @pl.loop(0, 8)
    def _(a):
        normed[a, :, 0:128] = norm_rows(mid[2 * a], p_gain)
        normed[a, :, 128:256] = norm_rows(mid[2 * a + 1], p_gain)
        edges(0, a)

    edges_send(0)

    @pl.loop(0, 8)
    def _(a):
        edges(1, a)

    edges_send(1)
    sent(r_all.at[pl.ds(0, 23), pl.ds(0, 256), :], e_ssem)

    @pl.loop(0, 8)
    def _(a):
        y = jax.nn.sigmoid(jnp.dot(wu[0], normed[a], preferred_element_type=F32))
        gate[2 * a] = y[:, :128]
        gate[2 * a + 1] = y[:, 128:]

    def t_copy(g, m):
        return remote(
            t_send.at[m // 2, m % 2, g], t_recv.at[m_own, g], t_ssem, t_rsem.at[g], zh * 16 + m
        )

    got = e_recv.reshape(2, 8, 2, 2, 8, 16, 128)
    for g in (0, 1):
        every = r_all.at[pl.ds(0, 23), pl.ds(0, 128), :]
        remote(every, every, e_ssem, e_rsem.at[g], sib).wait_recv()

        for c in range(4):
            t = None
            for hh in (0, 1):
                lhs = got[zh, :, hh, g, c].reshape(128, 128)
                rhs = got[:, :, hh, g, 4 + c].reshape(256, 128)
                term = lax.dot_general(lhs, rhs, NT, preferred_element_type=F32)
                t = term if t is None else t + term
            t = t.astype(BF16)
            for hh in (0, 1):
                t_send[:, hh, g, c] = t[:, hh * 128 : (hh + 1) * 128].reshape(8, 16, 128)

        @pl.loop(1, 16)
        def _(k):
            t_copy(g, (m_own + k) % 16).start()

        t_recv[m_own, g] = t_send[m_own // 2, h, g]

    sent(r_all.at[pl.ds(0, 15), pl.ds(0, 128), :], t_ssem)
    for g in (0, 1):
        fifteen = t_recv.at[pl.ds(0, 15), g]
        remote(fifteen, fifteen, t_ssem, t_rsem.at[g], sib).wait_recv()
        s_tri[g * 1024 : (g + 1) * 1024, :] = t_recv[:, g].reshape(1024, 128).astype(F32)


    def result(a):
        rows = [
            norm_rows(s_tri[pl.ds(2 * a + e, 128, stride=16), :], t_gain) for e in (0, 1)
        ]
        y = jnp.dot(wu[1], jnp.concatenate(rows, axis=1), preferred_element_type=F32)
        for e in (0, 1):
            i = 2 * a + e
            r = mid[i] + gate[i] * y[:, e * 128 : (e + 1) * 128]
            o_buf[i] = r.T.astype(BF16)

    @pl.loop(0, 4)
    def _(a):
        result(4 * (1 - h) + a)

    o_copy = remote(
        o_buf.at[pl.ds((1 - h) * 8, 8)], o_got, sib_send.at[3], sib_recv.at[3], sib
    )
    o_copy.start()
    pending.append(o_copy.wait_send)

    @pl.loop(0, 4)
    def _(a):
        result(4 * h + a)

    out[:, mine, :] = o_buf[pl.ds(h * 8, 8)]
    o_copy.wait_recv()
    out[:, other, :] = o_got[...]

    for wait in pending:
        wait()


def local(
    relative_embedding,
    coupling_features,
    relative_variance_multiplier,
    bilinear_lhs_projector,
    bilinear_rhs_projector,
    product_final_matrix,
    coupling_standard_scale,
    incoming_edge_matrix,
    incoming_edge_sigmoid,
    second_edge_matrix,
    second_edge_sigmoid,
    update_sigmoid_matrix,
    update_final_matrix,
    cubic_standard_scale,
):
    vm = pltpu.VMEM
    dma = pltpu.SemaphoreType.DMA
    return pl.pallas_call(
        kernel,
        out_shape=jax.ShapeDtypeStruct((8, 256, 128), BF16),
        in_specs=[pl.BlockSpec(memory_space=pl.ANY)] * 14,
        out_specs=pl.BlockSpec(memory_space=pltpu.VMEM),
        scratch_shapes=[
            vm((16, 256, 256), BF16),
            vm((1, 256), F32),
            vm((32, 256), BF16),
            vm((32, 256), BF16),
            vm((1024, 128), BF16),
            vm((2, 1, 128), F32),
            vm((6, 128, 128), BF16),
            vm((4096, 128), F32),
            vm((2, 512, 128), F32),
            vm((16, 16, 512), BF16),
            vm((16, 2, 16, 512), BF16),
            vm((512, 512), BF16),
            vm((32, 16, 128), BF16),
            vm((32, 512, 128), BF16),
            vm((16, ND, 32, 128), BF16),
            vm((16, 128, 128), BF16),
            vm((CHUNKS, 128, 128), BF16),
            vm((2, 256, 128), BF16),
            vm((2, 128, 128), BF16),
            vm((16, 128, 128), F32),
            vm((16, 128, 128), F32),
            vm((8, 128, 256), BF16),
            vm((1024, 128), F32),
            vm((1024, 128), F32),
            vm((16, 2, 8, 16, 128), BF16),
            vm((32, 2, 8, 16, 128), BF16),
            vm((8, 2, 2, 4, 16, 128), BF16),
            vm((16, 2, 4, 16, 128), BF16),
            vm((2048, 128), F32),
            vm((16, 128, 128), BF16),
            vm((8, 128, 128), BF16),
            dma((12,)),
            dma((4,)),
            dma((4,)),
            dma,
            dma,
            dma,
            dma,
            dma,
            dma((CHUNKS,)),
            dma((CHUNKS, 2)),
            dma((CHUNKS, 2)),
            dma,
            dma((2,)),
            dma,
            dma((2,)),
        ],
        compiler_params=pltpu.CompilerParams(
            collective_id=0, has_side_effects=True, vmem_limit_bytes=60 * 1024 * 1024
        ),
    )(
        relative_embedding,
        coupling_features,
        relative_variance_multiplier.reshape(1, -1),
        bilinear_lhs_projector.T,
        bilinear_rhs_projector.T,
        product_final_matrix,
        coupling_standard_scale.reshape(1, -1),
        incoming_edge_matrix,
        incoming_edge_sigmoid,
        second_edge_matrix,
        second_edge_sigmoid,
        update_sigmoid_matrix,
        update_final_matrix,
        cubic_standard_scale.reshape(1, -1),
    )


def solution(mesh):
    rows = P(("batch", "dap"), None, None)
    return jax.shard_map(
        local,
        mesh=mesh,
        in_specs=(rows, rows) + (P(),) * 12,
        out_specs=rows,
        check_vma=False,
    )
```

time: 108 us -> 100 us (0.926)
  Pallas kernels: 106 us -> 98 us
    pallas_call x1, Pallas kernels: 106 us -> 98 us  [local(): pl.pallas_call(kernel, out_shape=jax.ShapeDtypeStruct((8, 256, 128), BF16...]
where the time goes in v4:
time: 100 us; the launch traced here: 99.8 us
  Pallas kernels  98 us (98%)
  local copies, waits for them, and re-layouts  1.87 us (2%)
    pallas_call x1, Pallas kernels, local(): pl.pallas_call(kernel, out_shape=jax.ShapeDtypeStruct((8, 256, 128), BF16...  98 us

profile of v4, /device:TPU:1, one launch (start us, length us, event | category | flops | bytes accessed | tf_op | source)
XLA Modules:
  0.0 99.8 jit_solution(13447902449978001386)
XLA Ops:
  0.0 98.0 %shard_map.136 = bf16[8,256,128]{2,1,0:T(8,128)(2,1)} custom-call(bf16[16,256,256]{2,1,0:T(8,128)(2,1)} %msa_h.1, bf16[8,256,128]{2,1,0:T(8,128)(2,1)} %coup_h.1, f32[1,256]{1,0:T(1,128)} %bitcast.7, bf16[32,256]{1,0:T(8,128)(2,1)} %bitcast.5, bf16[32,256]{1,0:T(8,128)(2,1)} %bitcast.6, bf16[1024,128]{1,0:T(8,128)(2,1)} %w_final_h.1, f32[1,128]{1,0:T(1,128)} %bitcast.8, ...), custom_call_target="tpu_custom_call" | custom-call | tf_op jit(solution)/shard_map/pallas_call | solution.py:515
  98.0 1.9 %copy.16 = bf16[8,256,128]{2,1,0:T(8,128)(2,1)} copy(bf16[8,256,128]{2,1,0:T(8,128)(2,1)} %shard_map.136) | data formatting | bytes 1048576

commit v5 on v4

--- a/solution.py
+++ b/solution.py
@@ -1,3 +1,5 @@
+import functools
+
 import jax
 import jax.numpy as jnp
 from jax import lax
@@ -10,6 +12,7 @@
 BF16 = jnp.bfloat16
 CHUNKS = 8
 ND = 32 // CHUNKS
+GROUPS = (2, 4, 2)
 NT = (((1,), (1,)), ((), ()))
 
 
@@ -61,6 +64,7 @@
     s_left,
     s_right,
     l_send,
+    l_stage,
     l_all,
     l_t,
     r_send,
@@ -137,11 +141,11 @@
     pending = []
     barrier = pltpu.get_barrier_semaphore()
 
-    @pl.loop(1, 32)
-    def _(k):
-        pl.semaphore_signal(
-            barrier, inc=1, device_id={"dap": (me + k) % 32}, device_id_type=MESH
-        )
+    greeted = [sib]
+    for k in (1, 2, 3):
+        greeted += [dev((z + k) % 4, x), dev(z, (x + k) % 4)]
+    for to in greeted:
+        pl.semaphore_signal(barrier, inc=1, device_id={"dap": to}, device_id_type=MESH)
 
     for copy in first:
         copy.wait()
@@ -163,12 +167,34 @@
 
     for n in range(4):
         parts[n].wait()
-        pl.loop(4 * n, 4 * n + 4)(project)
+        pl.loop(4 * n, 4 * n + 4, unroll=2)(project)
 
     r_send[...] = s_right[1 - h].reshape(32, 16, 128).astype(BF16)
 
-    pl.semaphore_wait(barrier, 31)
-
+    lane = lax.broadcasted_iota(jnp.int32, (4, 16, 128), 2)
+
+    @pl.loop(0, 16, unroll=2)
+    def _(k):
+        v = s_left[pl.ds(pl.multiple_of(k * 256, 256), 256), :].reshape(4, 4, 16, 128)
+        v = jnp.where(
+            lane < 32,
+            v[:, 0],
+            jnp.where(lane < 64, v[:, 1], jnp.where(lane < 96, v[:, 2], v[:, 3])),
+        ).astype(BF16)
+        for g in range(4):
+            l_send[k, :, g * 128 : (g + 1) * 128] = v[g]
+
+    pl.semaphore_wait(barrier, 7)
+
+    def sent(ref, sem):
+        pending.append(remote(ref, ref, sem, sib_recv.at[0], sib).wait_send)
+
+    for k in (1, 2, 3):
+        z2 = (z + k) % 4
+        remote(
+            l_send.at[pl.ds(4 * z2, 4)], l_stage.at[z], l_ssem.at[0], l_rsem.at[0], dev(z2, x)
+        ).start()
+    sent(l_stage.at[pl.ds(0, 3)], l_ssem.at[0])
     my16 = pl.ds(pl.multiple_of((2 * pos + h) * 16, 16), 16)
     sib_r = remote(r_send, r_all.at[:, my16, :], sib_send.at[0], sib_recv.at[0], sib)
     sib_r.start()
@@ -224,9 +250,6 @@
         for k in (1, 2, 3):
             z_copy(c, k).start()
 
-    def sent(ref, sem):
-        pending.append(remote(ref, ref, sem, sib_recv.at[0], sib).wait_send)
-
     z_start(0)
 
     @pl.loop(0, CHUNKS)
@@ -235,36 +258,23 @@
             x_copy(c, z, n).start()
 
     z_start(1)
+    l_stage[z] = l_send[pl.ds(4 * z, 4)]
+    three = l_stage.at[pl.ds(0, 3)]
+    remote(three, three, l_ssem.at[0], l_rsem.at[0], sib).wait_recv()
+    for k in (1, 2, 3):
+        x2 = (x + k) % 4
+        remote(
+            l_stage.at[:, x2],
+            l_all.at[pl.ds(4 * x, 4), h],
+            l_ssem.at[1],
+            l_rsem.at[1],
+            dev(z, x2),
+        ).start()
+    sent(three, l_ssem.at[1])
+    l_all[pl.ds(4 * x, 4), h] = l_stage[:, x]
     sent(r_all.at[pl.ds(0, 3 * CHUNKS), pl.ds(0, 32 * ND), :], z_ssem)
     sent(r_all.at[pl.ds(0, 16)], x_ssem)
     sent(r_all.at[pl.ds(0, 8)], f_ssem)
-
-    lane = lax.broadcasted_iota(jnp.int32, (4, 16, 128), 2)
-
-    def l_copy(qq):
-        return remote(
-            l_send.at[qq], l_all.at[pos, h], l_ssem, l_rsem, 2 * qq + h
-        )
-
-    @pl.loop(0, 16)
-    def _(k):
-        qq = (q + k) % 16
-        v = s_left[pl.ds(pl.multiple_of(qq * 256, 256), 256), :].reshape(4, 4, 16, 128)
-        v = jnp.where(
-            lane < 32,
-            v[:, 0],
-            jnp.where(lane < 64, v[:, 1], jnp.where(lane < 96, v[:, 2], v[:, 3])),
-        ).astype(BF16)
-        for g in range(4):
-            l_send[qq, :, g * 128 : (g + 1) * 128] = v[g]
-
-        @pl.when(k > 0)
-        def _():
-            l_copy(qq).start()
-
-    l_all[pos, h] = l_send[q]
-
-    sent(l_all.at[pl.ds(0, 15), 0], l_ssem)
 
     def spread(c):
         z_wait(c)
@@ -291,7 +301,7 @@
             outer[:, 2 * p] = o[:, :128].reshape(16, 32, 128)
             outer[:, 2 * p + 1] = o[:, 128:].reshape(16, 32, 128)
 
-        @pl.loop(0, 8)
+        @pl.loop(0, 8, unroll=4)
         def _(a):
             rhs = jnp.concatenate(
                 [outer[2 * a].reshape(128, 128), outer[2 * a + 1].reshape(128, 128)], axis=1
@@ -313,8 +323,9 @@
         w2[b] = s_tri[1024 + b * 128 : 1024 + (b + 1) * 128, :].T.astype(BF16)
     for b in range(4):
         t = w_six[b].astype(F32).T.astype(BF16)
-        w5[0, b * 64 : (b + 1) * 64, :] = t[:64]
-        w5[1, b * 64 : (b + 1) * 64, :] = t[64:]
+        for g, n in enumerate(GROUPS):
+            lo, n = 16 * sum(GROUPS[:g]), 16 * n
+            w5[4 * lo + b * n : 4 * lo + (b + 1) * n, :] = t[lo : lo + n]
     for b in range(2):
         wu[b] = w_six[4 + b].astype(F32).T.astype(BF16)
     p_gain = column(gains[0])
@@ -335,14 +346,12 @@
         == lax.broadcasted_iota(jnp.int32, (128, 128), 1)
     ).astype(F32).astype(BF16)
 
-    @pl.loop(0, 16)
+    @pl.loop(0, 16, unroll=4)
     def _(i):
         mid[i] = lax.dot_general(eye, coup16[i], NT, preferred_element_type=F32)
 
     forward(1)
-    remote(
-        l_all.at[pl.ds(0, 15), h], l_all.at[pl.ds(0, 15), h], l_ssem, l_rsem, sib
-    ).wait_recv()
+    remote(three, three, l_ssem.at[1], l_rsem.at[1], sib).wait_recv()
     l_fwd = remote(l_all.at[:, h], l_all.at[:, h], sib_send.at[2], sib_recv.at[2], sib)
     l_fwd.start()
     pending.append(l_fwd.wait_send)
@@ -371,43 +380,48 @@
     m_own = me % 16
 
     def e_near(g, m):
-        return remote(e_send.at[m, g], e_recv.at[me, g], e_ssem, e_rsem.at[g], zh * 16 + m)
+        return remote(
+            e_send[g].at[m], e_recv[g].at[me], e_ssem, e_rsem.at[g], zh * 16 + m
+        )
 
     def e_far(g, m):
-        four = pl.ds(4, 4)
+        n = pl.ds(GROUPS[g], GROUPS[g])
         return remote(
-            e_send.at[m, g, four],
-            e_recv.at[me, g, four],
+            e_send[g].at[m, n],
+            e_recv[g].at[me, n],
             e_ssem,
             e_rsem.at[g],
             (1 - zh) * 16 + m,
         )
 
     def edges(g, a):
-        y = jnp.dot(w5[g], normed[a], preferred_element_type=F32)
-        el = jax.nn.sigmoid(y[64:128]) * y[0:64]
-        er = jax.nn.sigmoid(y[192:256]) * y[128:192]
+        lo, n = 64 * sum(GROUPS[:g]), 16 * GROUPS[g]
+        y = jnp.dot(w5[lo : lo + 4 * n], normed[a], preferred_element_type=F32)
+        el = jax.nn.sigmoid(y[n : 2 * n]) * y[0:n]
+        er = jax.nn.sigmoid(y[3 * n :]) * y[2 * n : 3 * n]
         for e in (0, 1):
-            rows = pl.ds(2 * a + e, 64, stride=16)
+            rows = pl.ds(2 * a + e, n, stride=16)
             s_el[rows, :] = el[:, e * 128 : (e + 1) * 128]
             s_er[rows, :] = er[:, e * 128 : (e + 1) * 128]
 
     def edges_send(g):
+        n = GROUPS[g]
+
         @pl.loop(0, 16)
         def _(k):
             m = (m_own + k) % 16
-            rows = pl.ds(pl.multiple_of(m * 64, 64), 64)
-            e_send[m, g, 0:4] = s_el[rows, :].reshape(4, 16, 128).astype(BF16)
-            e_send[m, g, 4:8] = s_er[rows, :].reshape(4, 16, 128).astype(BF16)
+            rows = pl.ds(pl.multiple_of(m * 16 * n, 16 * n), 16 * n)
+            e_send[g][m, 0:n] = s_el[rows, :].reshape(n, 16, 128).astype(BF16)
+            e_send[g][m, n : 2 * n] = s_er[rows, :].reshape(n, 16, 128).astype(BF16)
             e_far(g, m).start()
 
             @pl.when(k > 0)
             def _():
                 e_near(g, m).start()
 
-        e_recv[me, g] = e_send[m_own, g]
-
-    @pl.loop(0, 8)
+        e_recv[g][me] = e_send[g][m_own]
+
+    @pl.loop(0, 8, unroll=2)
     def _(a):
         normed[a, :, 0:128] = norm_rows(mid[2 * a], p_gain)
         normed[a, :, 128:256] = norm_rows(mid[2 * a + 1], p_gain)
@@ -415,11 +429,9 @@
 
     edges_send(0)
 
-    @pl.loop(0, 8)
-    def _(a):
-        edges(1, a)
-
-    edges_send(1)
+    for g in (1, 2):
+        pl.loop(0, 8, unroll=2)(functools.partial(edges, g))
+        edges_send(g)
     sent(r_all.at[pl.ds(0, 23), pl.ds(0, 256), :], e_ssem)
 
     @pl.loop(0, 8)
@@ -430,36 +442,41 @@
 
     def t_copy(g, m):
         return remote(
-            t_send.at[m // 2, m % 2, g], t_recv.at[m_own, g], t_ssem, t_rsem.at[g], zh * 16 + m
+            t_send[g].at[m // 2, m % 2],
+            t_recv[g].at[m_own],
+            t_ssem,
+            t_rsem.at[g],
+            zh * 16 + m,
         )
 
-    got = e_recv.reshape(2, 8, 2, 2, 8, 16, 128)
-    for g in (0, 1):
-        every = r_all.at[pl.ds(0, 23), pl.ds(0, 128), :]
+    for g, n in enumerate(GROUPS):
+        every = r_all.at[pl.ds(0, 23), pl.ds(0, 32 * n), :]
         remote(every, every, e_ssem, e_rsem.at[g], sib).wait_recv()
 
-        for c in range(4):
+        got = e_recv[g].reshape(2, 8, 2, 2 * n, 16, 128)
+        for c in range(n):
             t = None
             for hh in (0, 1):
-                lhs = got[zh, :, hh, g, c].reshape(128, 128)
-                rhs = got[:, :, hh, g, 4 + c].reshape(256, 128)
+                lhs = got[zh, :, hh, c].reshape(128, 128)
+                rhs = got[:, :, hh, n + c].reshape(256, 128)
                 term = lax.dot_general(lhs, rhs, NT, preferred_element_type=F32)
                 t = term if t is None else t + term
             t = t.astype(BF16)
             for hh in (0, 1):
-                t_send[:, hh, g, c] = t[:, hh * 128 : (hh + 1) * 128].reshape(8, 16, 128)
+                t_send[g][:, hh, c] = t[:, hh * 128 : (hh + 1) * 128].reshape(8, 16, 128)
 
         @pl.loop(1, 16)
         def _(k):
             t_copy(g, (m_own + k) % 16).start()
 
-        t_recv[m_own, g] = t_send[m_own // 2, h, g]
+        t_recv[g][m_own] = t_send[g][m_own // 2, h]
 
     sent(r_all.at[pl.ds(0, 15), pl.ds(0, 128), :], t_ssem)
-    for g in (0, 1):
-        fifteen = t_recv.at[pl.ds(0, 15), g]
+    for g, n in enumerate(GROUPS):
+        fifteen = t_recv[g].at[pl.ds(0, 15)]
         remote(fifteen, fifteen, t_ssem, t_rsem.at[g], sib).wait_recv()
-        s_tri[g * 1024 : (g + 1) * 1024, :] = t_recv[:, g].reshape(1024, 128).astype(F32)
+        lo = 256 * sum(GROUPS[:g])
+        s_tri[lo : lo + 256 * n, :] = t_recv[g][...].reshape(256 * n, 128).astype(F32)
 
 
     def result(a):
@@ -472,7 +489,7 @@
             r = mid[i] + gate[i] * y[:, e * 128 : (e + 1) * 128]
             o_buf[i] = r.T.astype(BF16)
 
-    @pl.loop(0, 4)
+    @pl.loop(0, 4, unroll=2)
     def _(a):
         result(4 * (1 - h) + a)
 
@@ -482,7 +499,7 @@
     o_copy.start()
     pending.append(o_copy.wait_send)
 
-    @pl.loop(0, 4)
+    @pl.loop(0, 4, unroll=2)
     def _(a):
         result(4 * h + a)
 
@@ -528,6 +545,7 @@
             vm((4096, 128), F32),
             vm((2, 512, 128), F32),
             vm((16, 16, 512), BF16),
+            vm((4, 4, 16, 512), BF16),
             vm((16, 2, 16, 512), BF16),
             vm((512, 512), BF16),
             vm((32, 16, 128), BF16),
@@ -535,25 +553,25 @@
             vm((16, ND, 32, 128), BF16),
             vm((16, 128, 128), BF16),
             vm((CHUNKS, 128, 128), BF16),
-            vm((2, 256, 128), BF16),
+            vm((512, 128), BF16),
             vm((2, 128, 128), BF16),
             vm((16, 128, 128), F32),
             vm((16, 128, 128), F32),
             vm((8, 128, 256), BF16),
             vm((1024, 128), F32),
             vm((1024, 128), F32),
-            vm((16, 2, 8, 16, 128), BF16),
-            vm((32, 2, 8, 16, 128), BF16),
-            vm((8, 2, 2, 4, 16, 128), BF16),
-            vm((16, 2, 4, 16, 128), BF16),
+            [vm((16, 2 * n, 16, 128), BF16) for n in GROUPS],
+            [vm((32, 2 * n, 16, 128), BF16) for n in GROUPS],
+            [vm((8, 2, n, 16, 128), BF16) for n in GROUPS],
+            [vm((16, n, 16, 128), BF16) for n in GROUPS],
             vm((2048, 128), F32),
             vm((16, 128, 128), BF16),
             vm((8, 128, 128), BF16),
             dma((12,)),
             dma((4,)),
             dma((4,)),
-            dma,
-            dma,
+            dma((2,)),
+            dma((2,)),
             dma,
             dma,
             dma,
@@ -561,9 +579,9 @@
             dma((CHUNKS, 2)),
             dma((CHUNKS, 2)),
             dma,
-            dma((2,)),
+            dma((3,)),
             dma,
-            dma((2,)),
+            dma((3,)),
         ],
         compiler_params=pltpu.CompilerParams(
             collective_id=0, has_side_effects=True, vmem_limit_bytes=60 * 1024 * 1024

time: 100 us -> 91.2 us (0.912)
  Pallas kernels: 98 us -> 89.2 us
    pallas_call x1, Pallas kernels: 98 us -> 89.2 us  [local(): pl.pallas_call(kernel, out_shape=jax.ShapeDtypeStruct((8, 256, 128), BF16...]
where the time goes in v5:
time: 91.2 us; the launch traced here: 91.1 us
  Pallas kernels  89.2 us (98%)
  local copies, waits for them, and re-layouts  1.87 us (2%)
    pallas_call x1, Pallas kernels, local(): pl.pallas_call(kernel, out_shape=jax.ShapeDtypeStruct((8, 256, 128), BF16...  89.2 us
    unnamed x1, local copies, waits for them, and re-layouts  1.87 us

profile of v5, /device:TPU:1, one launch (start us, length us, event | category | flops | bytes accessed | tf_op | source)
XLA Modules:
  0.0 91.1 jit_solution(1663738202474574377)
XLA Ops:
  0.0 89.2 %shard_map.136 = bf16[8,256,128]{2,1,0:T(8,128)(2,1)} custom-call(bf16[16,256,256]{2,1,0:T(8,128)(2,1)} %msa_h.1, bf16[8,256,128]{2,1,0:T(8,128)(2,1)} %coup_h.1, f32[1,256]{1,0:T(1,128)} %bitcast.7, bf16[32,256]{1,0:T(8,128)(2,1)} %bitcast.5, bf16[32,256]{1,0:T(8,128)(2,1)} %bitcast.6, bf16[1024,128]{1,0:T(8,128)(2,1)} %w_final_h.1, f32[1,128]{1,0:T(1,128)} %bitcast.8, ...), custom_call_target="tpu_custom_call" | custom-call | tf_op jit(solution)/shard_map/pallas_call | solution.py:532
  89.2 1.9 %copy.16 = bf16[8,256,128]{2,1,0:T(8,128)(2,1)} copy(bf16[8,256,128]{2,1,0:T(8,128)(2,1)} %shard_map.136) | data formatting | bytes 1048576

commit v6 on v5

--- a/solution.py
+++ b/solution.py
@@ -12,6 +12,7 @@
 BF16 = jnp.bfloat16
 CHUNKS = 8
 ND = 32 // CHUNKS
+LAST = CHUNKS - 1
 GROUPS = (2, 4, 2)
 NT = (((1,), (1,)), ((), ()))
 
@@ -95,6 +96,7 @@
     x_ssem,
     f_ssem,
     z_rsem,
+    e2_rsem,
     x_rsem,
     f_rsem,
     e_ssem,
@@ -195,8 +197,13 @@
             l_send.at[pl.ds(4 * z2, 4)], l_stage.at[z], l_ssem.at[0], l_rsem.at[0], dev(z2, x)
         ).start()
     sent(l_stage.at[pl.ds(0, 3)], l_ssem.at[0])
-    my16 = pl.ds(pl.multiple_of((2 * pos + h) * 16, 16), 16)
-    sib_r = remote(r_send, r_all.at[:, my16, :], sib_send.at[0], sib_recv.at[0], sib)
+    def part(c, hh):
+        rows = pl.ds(pl.multiple_of(32 * z + 16 * hh, 16), 16)
+        return r_all.at[pl.ds(c * ND, ND), x, rows, :]
+
+    all_mine = r_all.at[:, x, pl.ds(pl.multiple_of(32 * z + 16 * h, 16), 16), :]
+    all_other = r_all.at[:, x, pl.ds(pl.multiple_of(32 * z + 16 * (1 - h), 16), 16), :]
+    sib_r = remote(r_send, all_mine, sib_send.at[0], sib_recv.at[0], sib)
     sib_r.start()
     sib_c = remote(
         coup_h.at[:, other, :],
@@ -207,20 +214,29 @@
     )
     sib_c.start()
     pending += [sib_r.wait_send, sib_c.wait_send]
-    r_all[:, my16, :] = s_right[h].reshape(32, 16, 128).astype(BF16)
-
-    sib16 = pl.ds(pl.multiple_of((2 * pos + 1 - h) * 16, 16), 16)
-    remote(r_send, r_all.at[:, sib16, :], sib_send.at[0], sib_recv.at[0], sib).wait_recv()
+    all_mine[...] = s_right[h].reshape(32, 16, 128).astype(BF16)
 
     def block(c, zz, xx):
-        rows = pl.ds(pl.multiple_of((4 * xx + zz) * 32, 32), 32)
-        return r_all.at[pl.ds(c * ND, ND), rows, :]
+        rows = pl.ds(pl.multiple_of(32 * zz, 32), 32)
+        return r_all.at[pl.ds(c * ND, ND), xx, rows, :]
 
     def blocks(c, xx, half=None):
-        rows = pl.ds(pl.multiple_of(xx * 128, 128), 128)
         if half is None:
-            return r_all.at[pl.ds(c * ND, ND), rows, :]
-        return r_all.at[pl.ds(c * ND + half * (ND // 2), ND // 2), rows, :]
+            return r_all.at[pl.ds(c * ND, ND), xx]
+        return r_all.at[pl.ds(c * ND + half * (ND // 2), ND // 2), xx]
+
+    def row(zz):
+        rows = pl.ds(pl.multiple_of(32 * zz, 32), 32)
+        return r_all.at[pl.ds(LAST * ND, ND), :, rows, :]
+
+    def row_half(xx, half):
+        rows = pl.ds(pl.multiple_of(32 * z, 32), 32)
+        return r_all.at[pl.ds(LAST * ND + half * (ND // 2), ND // 2), xx, rows, :]
+
+    def own_start(c, hh):
+        for n in (0, 1):
+            b = part(c, hh)
+            remote(b, b, x_ssem, x_rsem.at[c, n], dev(z, (x + 1 + 2 * n) % 4)).start()
 
     def z_copy(c, k):
         b = block(c, z, x)
@@ -234,9 +250,17 @@
         b = blocks(c, (x + 3 - 2 * n) % 4, n)
         return remote(b, b, f_ssem, f_rsem.at[c, n], dev(z, (x + 1 + 2 * n) % 4))
 
-    def z_wait(c):
-        three = r_all.at[pl.ds(c * ND, ND), pl.ds(0, 96), :]
-        remote(three, three, z_ssem, z_rsem.at[c], sib).wait_recv()
+    at_end = z % 3 == 0
+    inner = z % 3 != 0
+    end = 3 * (z // 2)
+
+    def z_relay(c):
+        b = block(c, 3 - end, x)
+        return remote(b, b, z_ssem, e2_rsem.at[c], dev(end, x))
+
+    def z_wait(c, n):
+        b = r_all.at[pl.ds(c * ND, ND), 0, pl.ds(0, 32 * n), :]
+        remote(b, b, z_ssem, z_rsem.at[c], sib).wait_recv()
 
     def x_wait(c, n):
         b = blocks(c, (x + 3 - 2 * n) % 4)
@@ -248,14 +272,60 @@
 
     def z_start(c):
         for k in (1, 2, 3):
-            z_copy(c, k).start()
-
+
+            @pl.when(((z + k) % 4 - z) * ((z + k) % 4 - z) < 9)
+            def _():
+                z_copy(c, k).start()
+
+    def row_start():
+        for k in (1, 2, 3):
+            to = (z + k) % 4
+
+            @pl.when((to - z) * (to - z) < 9)
+            def _():
+                remote(row(z), row(z), z_ssem, z_rsem.at[LAST], dev(to, x)).start()
+
+    def row_forward():
+        for n in (0, 1):
+            b = block(LAST, z, (x + 3 - 2 * n) % 4)
+            remote(b, b, x_ssem, x_rsem.at[LAST, n], sib).wait_recv()
+            b = row_half((x + 3 - 2 * n) % 4, n)
+            remote(b, b, f_ssem, f_rsem.at[LAST, n], dev(z, (x + 1 + 2 * n) % 4)).start()
+
+    def row_forwarded():
+        for n in (0, 1):
+            b = row_half((x + 2) % 4, n)
+            remote(b, b, f_ssem, f_rsem.at[LAST, n], sib).wait_recv()
+
+    def row_relay():
+        @pl.when(inner)
+        def _():
+            ref = r_all.at[pl.ds(0, 3 * ND), 0]
+            remote(ref, ref, z_ssem, z_rsem.at[LAST], sib).wait_recv()
+            b = row(3 - end)
+            remote(b, b, z_ssem, e2_rsem.at[LAST], dev(end, x)).start()
+
+        @pl.when(at_end)
+        def _():
+            ref = r_all.at[pl.ds(0, 2 * ND), 0]
+            remote(ref, ref, z_ssem, z_rsem.at[LAST], sib).wait_recv()
+
+    def row_relayed():
+        @pl.when(at_end)
+        def _():
+            b = row(3 - z)
+            remote(b, b, z_ssem, e2_rsem.at[LAST], sib).wait_recv()
+
+    @pl.loop(0, CHUNKS)
+    def _(k):
+        own_start((k + LAST) % CHUNKS, h)
+
+    remote(r_send, all_other, sib_send.at[0], sib_recv.at[0], sib).wait_recv()
     z_start(0)
 
     @pl.loop(0, CHUNKS)
-    def _(c):
-        for n in (0, 1):
-            x_copy(c, z, n).start()
+    def _(k):
+        own_start((k + LAST) % CHUNKS, 1 - h)
 
     z_start(1)
     l_stage[z] = l_send[pl.ds(4 * z, 4)]
@@ -272,17 +342,46 @@
         ).start()
     sent(three, l_ssem.at[1])
     l_all[pl.ds(4 * x, 4), h] = l_stage[:, x]
-    sent(r_all.at[pl.ds(0, 3 * CHUNKS), pl.ds(0, 32 * ND), :], z_ssem)
-    sent(r_all.at[pl.ds(0, 16)], x_ssem)
-    sent(r_all.at[pl.ds(0, 8)], f_ssem)
+
+    def z_sent():
+        for here, n in ((at_end, 2), (inner, 4)):
+
+            @pl.when(here)
+            def _():
+                ref = r_all.at[pl.ds(0, CHUNKS + 3), pl.ds(0, n)]
+                remote(ref, ref, z_ssem, sib_recv.at[0], sib).wait_send()
+
+    pending.append(z_sent)
+    sent(r_all.at[pl.ds(0, 4 * LAST + 1), pl.ds(0, 2)], x_ssem)
+    sent(r_all.at[pl.ds(0, 4 * LAST + 1), 0], f_ssem)
 
     def spread(c):
-        z_wait(c)
+        @pl.when(inner)
+        def _():
+            z_wait(c, 3)
+            z_relay(c).start()
+
+        @pl.when(at_end)
+        def _():
+            z_wait(c, 2)
+
+        if c + 2 < LAST:
+            z_start(c + 2)
         for k in (1, 2, 3):
+            zz = (z + k) % 4
+
+            @pl.when((zz - z) * (zz - z) < 9)
+            def _():
+                for n in (0, 1):
+                    x_copy(c, zz, n).start()
+
+    def spread_end(c):
+        @pl.when(at_end)
+        def _():
+            b = block(c, 3 - z, x)
+            remote(b, b, z_ssem, e2_rsem.at[c], sib).wait_recv()
             for n in (0, 1):
-                x_copy(c, (z + k) % 4, n).start()
-        if c + 2 < CHUNKS:
-            z_start(c + 2)
+                x_copy(c, 3 - z, n).start()
 
     def forward(c):
         for n in (0, 1):
@@ -290,12 +389,17 @@
             f_copy(c, n).start()
 
     def finish(c):
-        for n in (0, 1):
-            f_wait(c, n)
+        if c == LAST:
+            row_relayed()
+        else:
+            for n in (0, 1):
+                f_wait(c, n)
 
         for p in range(ND // 2):
             d = c * ND + 2 * p
-            rhs = jnp.concatenate([r_all[d], r_all[d + 1]], axis=1)
+            rhs = jnp.concatenate(
+                [r_all[d].reshape(512, 128), r_all[d + 1].reshape(512, 128)], axis=1
+            )
             o = jnp.dot(l_t[...], rhs, preferred_element_type=F32) * (1.0 / 512)
             o = o.astype(BF16)
             outer[:, 2 * p] = o[:, :128].reshape(16, 32, 128)
@@ -311,7 +415,10 @@
             mid[2 * a + 1] += u[:, 128:]
 
     spread(0)
+    spread_end(0)
     spread(1)
+    spread_end(1)
+    row_forward()
 
     for copy in later:
         copy.wait()
@@ -333,6 +440,7 @@
 
     spread(2)
     forward(0)
+    spread_end(2)
 
     remote(
         coup_h.at[:, other, :],
@@ -356,6 +464,7 @@
     l_fwd.start()
     pending.append(l_fwd.wait_send)
     spread(3)
+    spread_end(3)
     remote(
         l_all.at[:, 1 - h], l_all.at[:, 1 - h], sib_send.at[2], sib_recv.at[2], sib
     ).wait_recv()
@@ -365,15 +474,21 @@
         )
 
     finish(0)
-    forward(2)
-    finish(1)
-    for c in range(4, CHUNKS):
+    row_forwarded()
+    for c in range(4, LAST):
         spread(c)
-        forward(c - 1)
-        finish(c - 2)
-    forward(CHUNKS - 1)
-    finish(CHUNKS - 2)
-    finish(CHUNKS - 1)
+        if c == 4:
+            row_start()
+        spread_end(c)
+        forward(c - 2)
+        finish(c - 3)
+    row_relay()
+    forward(LAST - 2)
+    finish(LAST - 3)
+    forward(LAST - 1)
+    finish(LAST)
+    finish(LAST - 2)
+    finish(LAST - 1)
 
 
     zh = me // 16
@@ -432,7 +547,7 @@
     for g in (1, 2):
         pl.loop(0, 8, unroll=2)(functools.partial(edges, g))
         edges_send(g)
-    sent(r_all.at[pl.ds(0, 23), pl.ds(0, 256), :], e_ssem)
+    sent(r_all.at[pl.ds(0, 23), pl.ds(0, 2)], e_ssem)
 
     @pl.loop(0, 8)
     def _(a):
@@ -450,7 +565,7 @@
         )
 
     for g, n in enumerate(GROUPS):
-        every = r_all.at[pl.ds(0, 23), pl.ds(0, 32 * n), :]
+        every = r_all.at[pl.ds(0, 23), 0, pl.ds(0, 32 * n), :]
         remote(every, every, e_ssem, e_rsem.at[g], sib).wait_recv()
 
         got = e_recv[g].reshape(2, 8, 2, 2 * n, 16, 128)
@@ -471,7 +586,7 @@
 
         t_recv[g][m_own] = t_send[g][m_own // 2, h]
 
-    sent(r_all.at[pl.ds(0, 15), pl.ds(0, 128), :], t_ssem)
+    sent(r_all.at[pl.ds(0, 15), 0], t_ssem)
     for g, n in enumerate(GROUPS):
         fifteen = t_recv[g].at[pl.ds(0, 15)]
         remote(fifteen, fifteen, t_ssem, t_rsem.at[g], sib).wait_recv()
@@ -549,7 +664,7 @@
             vm((16, 2, 16, 512), BF16),
             vm((512, 512), BF16),
             vm((32, 16, 128), BF16),
-            vm((32, 512, 128), BF16),
+            vm((32, 4, 128, 128), BF16),
             vm((16, ND, 32, 128), BF16),
             vm((16, 128, 128), BF16),
             vm((CHUNKS, 128, 128), BF16),
@@ -575,6 +690,7 @@
             dma,
             dma,
             dma,
+            dma((CHUNKS,)),
             dma((CHUNKS,)),
             dma((CHUNKS, 2)),
             dma((CHUNKS, 2)),

time: 91.2 us -> 89.2 us (0.978)
  Pallas kernels: 89.2 us -> 87.2 us
    pallas_call x1, Pallas kernels: 89.2 us -> 87.2 us  [local(): pl.pallas_call(kernel, out_shape=jax.ShapeDtypeStruct((8, 256, 128), BF16...]
where the time goes in v6:
time: 89.2 us; the launch traced here: 89 us
  Pallas kernels  87.2 us (98%)
  local copies, waits for them, and re-layouts  1.87 us (2%)
    pallas_call x1, Pallas kernels, local(): pl.pallas_call(kernel, out_shape=jax.ShapeDtypeStruct((8, 256, 128), BF16...  87.2 us
    unnamed x1, local copies, waits for them, and re-layouts  1.87 us

profile of v6, /device:TPU:1, one launch (start us, length us, event | category | flops | bytes accessed | tf_op | source)
XLA Modules:
  0.0 89.0 jit_solution(14431633324805343940)
XLA Ops:
  0.0 87.2 %shard_map.136 = bf16[8,256,128]{2,1,0:T(8,128)(2,1)} custom-call(bf16[16,256,256]{2,1,0:T(8,128)(2,1)} %msa_h.1, bf16[8,256,128]{2,1,0:T(8,128)(2,1)} %coup_h.1, f32[1,256]{1,0:T(1,128)} %bitcast.7, bf16[32,256]{1,0:T(8,128)(2,1)} %bitcast.5, bf16[32,256]{1,0:T(8,128)(2,1)} %bitcast.6, bf16[1024,128]{1,0:T(8,128)(2,1)} %w_final_h.1, f32[1,128]{1,0:T(1,128)} %bitcast.8, ...), custom_call_target="tpu_custom_call" | custom-call | tf_op jit(solution)/shard_map/pallas_call | solution.py:647
  87.2 1.9 %copy.16 = bf16[8,256,128]{2,1,0:T(8,128)(2,1)} copy(bf16[8,256,128]{2,1,0:T(8,128)(2,1)} %shard_map.136) | data formatting | bytes 1048576

commit v7 on v6

--- a/solution.py
+++ b/solution.py
@@ -13,7 +13,7 @@
 CHUNKS = 8
 ND = 32 // CHUNKS
 LAST = CHUNKS - 1
-GROUPS = (2, 4, 2)
+GROUPS = (2, 3, 2, 1)
 NT = (((1,), (1,)), ((), ()))
 
 
@@ -405,7 +405,7 @@
             outer[:, 2 * p] = o[:, :128].reshape(16, 32, 128)
             outer[:, 2 * p + 1] = o[:, 128:].reshape(16, 32, 128)
 
-        @pl.loop(0, 8, unroll=4)
+        @pl.loop(0, 8, unroll=8)
         def _(a):
             rhs = jnp.concatenate(
                 [outer[2 * a].reshape(128, 128), outer[2 * a + 1].reshape(128, 128)], axis=1
@@ -544,7 +544,7 @@
 
     edges_send(0)
 
-    for g in (1, 2):
+    for g in range(1, len(GROUPS)):
         pl.loop(0, 8, unroll=2)(functools.partial(edges, g))
         edges_send(g)
     sent(r_all.at[pl.ds(0, 23), pl.ds(0, 2)], e_ssem)
@@ -695,9 +695,9 @@
             dma((CHUNKS, 2)),
             dma((CHUNKS, 2)),
             dma,
-            dma((3,)),
+            dma((len(GROUPS),)),
             dma,
-            dma((3,)),
+            dma((len(GROUPS),)),
         ],
         compiler_params=pltpu.CompilerParams(
             collective_id=0, has_side_effects=True, vmem_limit_bytes=60 * 1024 * 1024

time: 89.2 us -> 88.2 us (0.989)
  Pallas kernels: 87.2 us -> 86.2 us
    pallas_call x1, Pallas kernels: 87.2 us -> 86.2 us  [local(): pl.pallas_call(kernel, out_shape=jax.ShapeDtypeStruct((8, 256, 128), BF16...]
where the time goes in v7:
time: 88.2 us; the launch traced here: 88.1 us
  Pallas kernels  86.2 us (98%)
  local copies, waits for them, and re-layouts  1.87 us (2%)
    pallas_call x1, Pallas kernels, local(): pl.pallas_call(kernel, out_shape=jax.ShapeDtypeStruct((8, 256, 128), BF16...  86.2 us
    unnamed x1, local copies, waits for them, and re-layouts  1.87 us

profile of v7, /device:TPU:1, one launch (start us, length us, event | category | flops | bytes accessed | tf_op | source)
XLA Modules:
  0.0 88.1 jit_solution(6330483176899837463)
XLA Ops:
  0.0 86.2 %shard_map.136 = bf16[8,256,128]{2,1,0:T(8,128)(2,1)} custom-call(bf16[16,256,256]{2,1,0:T(8,128)(2,1)} %msa_h.1, bf16[8,256,128]{2,1,0:T(8,128)(2,1)} %coup_h.1, f32[1,256]{1,0:T(1,128)} %bitcast.7, bf16[32,256]{1,0:T(8,128)(2,1)} %bitcast.5, bf16[32,256]{1,0:T(8,128)(2,1)} %bitcast.6, bf16[1024,128]{1,0:T(8,128)(2,1)} %w_final_h.1, f32[1,128]{1,0:T(1,128)} %bitcast.8, ...), custom_call_target="tpu_custom_call" | custom-call | tf_op jit(solution)/shard_map/pallas_call | solution.py:647
  86.2 1.9 %copy.16 = bf16[8,256,128]{2,1,0:T(8,128)(2,1)} copy(bf16[8,256,128]{2,1,0:T(8,128)(2,1)} %shard_map.136) | data formatting | bytes 1048576
